TPU v7x, 256 devices: a whole 4x4x8 slice. The times are simulated.
256 devices in a mesh: dp: 4 (over x), lat: 64 (over z, y, core).
Axes of the slice: x: 4, y: 4, z: 8, core: 2. Of those that a mesh axis runs over, the one named last changes fastest.
Arguments:
- state: float32 [32, 128, 256, 128], P('dp', 'lat'), may hold values from -8 to 8
- forcing: bfloat16 [32, 128, 256, 128], P('dp', 'lat'), may hold values from -6 to 6
- state_cot: float32 [32, 128, 256, 128], P('dp', 'lat'), may hold values from -8 to 8
- mat_master: float32 [327680], P(('dp', 'lat'))
- mat_moment: float32 [327680], P(('dp', 'lat')), may hold values from -0.0012207031 to 0.0012207031
- mat_second: float32 [327680], P(('dp', 'lat')), may hold values from 1.5993163e-07 to 6.397265e-07
- bias_master: float32 [1408], replicated, may hold values from -1.75 to 1.75
- bias_moment: float32 [1408], replicated, may hold values from -0.0012207031 to 0.0012207031
- bias_second: float32 [1408], replicated, may hold values from 1.5993163e-07 to 6.397265e-07
- level_coupling: float32 [128, 128], replicated, may hold values from -0.5 to 0.5
- lat_of_row: int32 [128], replicated, may hold values from 0 to 127, each once
- step_count: int32 [1], replicated, may hold values from 2 to 20
Outputs:
- state_out: float32 [32, 128, 256, 128], P('dp', 'lat')
- state_grad: float32 [32, 128, 256, 128], P('dp', 'lat')
- mat_grad: float32 [327680], P(('dp', 'lat'))
- mat_new: float32 [327680], P(('dp', 'lat'))
- mat_copy: bfloat16 [327680], P(('dp', 'lat'))
- mat_moment_new: float32 [327680], P(('dp', 'lat'))
- mat_second_new: float32 [327680], P(('dp', 'lat'))
- bias_grad: float32 [1408], replicated
- bias_new: float32 [1408], replicated
- bias_moment_new: float32 [1408], replicated
- bias_second_new: float32 [1408], replicated
- grad_norm: float32 [1], replicated
Inputs may be any that keep to these rules, and one draw needn't show every extreme that they name: `lat_of_row`: each latitude index names exactly one stored row.
All inputs are finite; a program needn't handle non-finite values.
Results may differ from a plain program's by a relative error of at most 0.0095.
Values may be sent and summed in bfloat16 or wider, within the bound.
A program may use at most 128 MiB of HBM per device.

v0:
```python
import math

import jax
import jax.numpy as jnp
from jax import lax
from jax.sharding import PartitionSpec as P

C = 128
F = 128
H = 256
NLAT = 128
NLON = 256
MW = 128
MB = 4


beta_one = 0.9
beta_two = 0.95
learn_rate = 0.3
decay_rate = 0.1
adam_eps = 1e-08
clip_norm = 1.0


def as_sent(shard):

    def short(part):
        return part.astype(jnp.bfloat16) if part.dtype == jnp.float32 else part

    return jax.tree.map(short, shard)


def unpack(flat):
    shapes = [(C, C), (C + F, H), (H, H), (H, H), (H, H), (H, C), (C, C)]
    pieces = []
    offset = 0
    for height, breadth in shapes:
        pieces.append(flat[offset : offset + height * breadth].reshape(height, breadth))
        offset += height * breadth
    return pieces


def split_bias(vector):
    return jnp.split(vector, [C, C + H, C + 2 * H, C + 3 * H, C + 4 * H, 2 * C + 4 * H])


def legendre_table(wavenumber, sine_lat, cosine_lat, total_waves):
    k_values = jnp.arange(1, total_waves, dtype=jnp.float32)
    log_terms = jnp.log((2.0 * k_values + 1.0) / (2.0 * k_values))
    below_mask = (k_values[None, :] <= wavenumber[:, None]).astype(jnp.float32)
    log_start = -0.5 * math.log(2.0) + 0.5 * jnp.sum(below_mask * log_terms[None, :], axis=1)
    initial = jnp.exp(log_start[:, None] + wavenumber[:, None] * jnp.log(cosine_lat)[None, :])

    def advance(state_pair, offset):
        latest, earlier = state_pair
        degree = wavenumber + offset
        degree_less = degree - 1.0
        factor_up = jnp.sqrt(
            (4.0 * degree * degree - 1.0) / (degree * degree - wavenumber * wavenumber)
        )
        factor_down = jnp.sqrt(
            jnp.maximum(
                (degree_less * degree_less - wavenumber * wavenumber)
                / (4.0 * degree_less * degree_less - 1.0),
                0.0,
            )
        )
        computed = factor_up[:, None] * (
            sine_lat[None, :] * latest - factor_down[:, None] * earlier
        )
        return ((computed, latest), computed)

    offsets = jnp.arange(1, total_waves, dtype=jnp.float32)
    final_pair, stacked = lax.scan(advance, (initial, jnp.zeros_like(initial)), offsets)
    return jnp.concatenate([initial[:, None, :], jnp.moveaxis(stacked, 0, 1)], axis=1)


def grid_tables(slot_ids, total_waves, lon_count):
    live_mask = (slot_ids < total_waves).astype(jnp.float32)
    longitude = jnp.arange(lon_count, dtype=jnp.int32)
    turns = slot_ids[:, None] * longitude[None, :] % lon_count
    angles = turns.astype(jnp.float32) * (2.0 * math.pi / lon_count)
    cosine_vals = jnp.cos(angles)
    sine_vals = jnp.sin(angles)
    forward_scale = live_mask / lon_count
    analysis = jnp.stack(
        [cosine_vals.T * forward_scale[None, :], -sine_vals.T * forward_scale[None, :]], axis=2
    ).reshape(lon_count, -1)
    weight_m = jnp.where(slot_ids == 0, 1.0, 2.0) * live_mask
    synthesis = jnp.stack(
        [cosine_vals * weight_m[:, None], -sine_vals * weight_m[:, None]], axis=1
    ).reshape(-1, lon_count)
    return (analysis, synthesis)


def spectral_tables(wave_ids, lat_of_row, total_waves, nlat_count):
    live_mask = wave_ids < total_waves
    wavenumber = jnp.minimum(wave_ids, total_waves - 1).astype(jnp.float32)
    angles = (lat_of_row.astype(jnp.float32) + 0.5) * (math.pi / nlat_count) - 0.5 * math.pi
    sine_lat = jnp.sin(angles)
    cosine_lat = jnp.cos(angles)
    poly = legendre_table(wavenumber, sine_lat, cosine_lat, total_waves)
    degree = wavenumber[:, None] + jnp.arange(total_waves, dtype=jnp.float32)[None, :]
    valid = (live_mask[:, None] & (degree < total_waves - 0.5)).astype(jnp.float32)
    synth_leg = poly * valid[:, :, None]
    quadrature = math.pi / nlat_count * cosine_lat
    anal_leg = synth_leg * quadrature[None, None, :]
    tendency = degree * (degree + 1.0) / (total_waves * (total_waves - 1.0))
    filt = jnp.exp(-((degree / total_waves) ** 8)) * valid
    return (anal_leg, synth_leg, tendency, filt)


def adam_update(weights, moment, second, grads, steps_done):
    moment_new = beta_one * moment + (1.0 - beta_one) * grads
    second_new = beta_two * second + (1.0 - beta_two) * grads * grads
    moment_hat = moment_new / (1.0 - beta_one**steps_done)
    second_hat = second_new / (1.0 - beta_two**steps_done)
    weights_new = weights - learn_rate * (
        moment_hat / (jnp.sqrt(second_hat) + adam_eps) + decay_rate * weights
    )
    return (weights_new, moment_new, second_new)


def weight_grad(inputs_low, grads_low):
    return lax.dot_general(
        inputs_low, grads_low, (((0,), (0,)), ((), ())), preferred_element_type=jnp.float32
    )


def back_prod(grads_low, matrix):
    return lax.dot_general(
        grads_low, matrix, (((1,), (1,)), ((), ())), preferred_element_type=jnp.float32
    )


def gelu_back(pre_act, upstream):
    outputs, pullback = jax.vjp(jax.nn.gelu, pre_act)
    return pullback(upstream)[0]


def dynamics_local(spec_in, anal_leg, synth_leg, filt_full, tend_full, coupling, slots_dev):
    high = lax.Precision.HIGHEST
    globes = spec_in.shape[0]
    spec = spec_in.reshape(globes, NLAT, slots_dev, 2, C)
    coef = jnp.einsum("snj,gjsqc->gsnqc", anal_leg, spec, precision=high)
    mixed = jnp.einsum("gsnqc,cd->gsnqd", coef, coupling, precision=high)
    coef_new = filt_full * (coef - tend_full * mixed)
    return jnp.einsum("snj,gsnqc->gjsqc", synth_leg, coef_new, precision=high).reshape(
        globes, NLAT, 2 * slots_dev, C
    )


def adjoint_local(back_in, anal_leg, synth_leg, filt_full, tend_full, coupling, slots_dev):
    high = lax.Precision.HIGHEST
    globes = back_in.shape[0]
    back_spec = back_in.reshape(globes, NLAT, slots_dev, 2, C)
    back_coef_new = jnp.einsum("snj,gjsqc->gsnqc", synth_leg, back_spec, precision=high)
    filtered = filt_full * back_coef_new
    back_coef = filtered - jnp.einsum(
        "gsnqd,cd->gsnqc", tend_full * filtered, coupling, precision=high
    )
    return jnp.einsum("snj,gsnqc->gjsqc", anal_leg, back_coef, precision=high).reshape(
        globes, NLAT, 2 * slots_dev, C
    )


def local(
    state,
    forcing,
    state_cot,
    mat_master,
    mat_moment,
    mat_second,
    bias_master,
    bias_moment,
    bias_second,
    level_coupling,
    lat_of_row,
    step_count,
):
    high = lax.Precision.HIGHEST
    lat_devices = lax.axis_size("lat")
    slots_dev = (MW + lat_devices - 1) // lat_devices
    slot_total = slots_dev * lat_devices
    analysis, synthesis = grid_tables(jnp.arange(slot_total, dtype=jnp.int32), MW, NLON)
    own_slots = lax.axis_index("lat") * slots_dev + jnp.arange(slots_dev, dtype=jnp.int32)
    anal_leg, synth_leg, tendency, filt = spectral_tables(own_slots, lat_of_row, MW, NLAT)
    filt_full = filt[None, :, :, None, None]
    tend_full = tendency[None, :, :, None, None]
    tables = (anal_leg, synth_leg, filt_full, tend_full, level_coupling, slots_dev)
    globes = state.shape[0] // MB
    row_count = state.shape[1]
    columns = globes * row_count * NLON
    biases = split_bias(bias_master)
    master_low = mat_master.astype(jnp.bfloat16)
    mats_list = []
    rows_list = []
    four_list = []
    for micro_step in range(MB):
        gathered = lax.all_gather(master_low, ("dp", "lat"), axis=0, tiled=True)
        mats = unpack(gathered)
        mats_list.append(mats)
        first_globe = micro_step * globes
        rows_in = state[first_globe : first_globe + globes].reshape(columns, C)
        rows_low = rows_in.astype(jnp.bfloat16)
        rows_list.append(rows_low)
        encoded = (
            rows_in + jnp.dot(rows_low, mats[0], preferred_element_type=jnp.float32) + biases[0]
        )
        four_list.append(
            jnp.einsum(
                "gric,ik->grkc",
                encoded.reshape(globes, row_count, NLON, C),
                analysis,
                precision=high,
            )
        )
    grid_list = []
    for micro_step in range(MB):
        spec_in = lax.all_to_all(
            four_list[micro_step].astype(jnp.bfloat16),
            "lat",
            split_axis=2,
            concat_axis=1,
            tiled=True,
        ).astype(jnp.float32)
        grid_list.append(
            lax.all_to_all(
                as_sent(dynamics_local(spec_in, *tables)),
                "lat",
                split_axis=1,
                concat_axis=2,
                tiled=True,
            )
        )
    mat_total = jnp.zeros(mat_master.shape, jnp.float32)
    bias_total = jnp.zeros(bias_master.shape, jnp.float32)
    state_pieces = []
    partial_grads = []
    back_list = []
    for micro_step in range(MB):
        mats = mats_list[micro_step]
        first_globe = micro_step * globes
        forcing_now = forcing[first_globe : first_globe + globes].reshape(columns, F)
        upstream = state_cot[first_globe : first_globe + globes].reshape(columns, C)
        dynamic = jnp.einsum(
            "grkc,ki->gric", grid_list[micro_step], synthesis, precision=high
        ).reshape(columns, C)
        hidden = jnp.concatenate([dynamic.astype(jnp.bfloat16), forcing_now], axis=1)
        kept_inputs = [hidden]
        kept_pre = []
        for layer_id in range(4):
            pre_act = (
                jnp.dot(hidden, mats[1 + layer_id], preferred_element_type=jnp.float32)
                + biases[1 + layer_id]
            )
            kept_pre.append(pre_act)
            hidden = jax.nn.gelu(pre_act).astype(jnp.bfloat16)
            kept_inputs.append(hidden)
        middle = dynamic + jnp.dot(hidden, mats[5], preferred_element_type=jnp.float32) + biases[5]
        middle_low = middle.astype(jnp.bfloat16)
        output = (
            middle + jnp.dot(middle_low, mats[6], preferred_element_type=jnp.float32) + biases[6]
        )
        state_pieces.append(output.reshape(globes, row_count, NLON, C))
        grad_list = [None] * 7
        bias_parts = [None] * 7
        up_low = upstream.astype(jnp.bfloat16)
        grad_list[6] = weight_grad(middle_low, up_low)
        bias_parts[6] = jnp.sum(upstream, axis=0)
        back_mid = upstream + back_prod(up_low, mats[6])
        mid_low = back_mid.astype(jnp.bfloat16)
        grad_list[5] = weight_grad(kept_inputs[4], mid_low)
        bias_parts[5] = jnp.sum(back_mid, axis=0)
        back_hidden = back_prod(mid_low, mats[5])
        for layer_id in (3, 2, 1, 0):
            back_pre = gelu_back(kept_pre[layer_id], back_hidden)
            pre_low = back_pre.astype(jnp.bfloat16)
            grad_list[1 + layer_id] = weight_grad(kept_inputs[layer_id], pre_low)
            bias_parts[1 + layer_id] = jnp.sum(back_pre, axis=0)
            weight_now = mats[1 + layer_id]
            if layer_id == 0:
                weight_now = weight_now[:C]
            back_hidden = back_prod(pre_low, weight_now)
        back_dyn = (back_mid + back_hidden).reshape(globes, row_count, NLON, C)
        back_list.append(jnp.einsum("gric,ki->grkc", back_dyn, synthesis, precision=high))
        partial_grads.append((grad_list, bias_parts))
    back_rows_list = []
    for micro_step in range(MB):
        back_spec = lax.all_to_all(
            back_list[micro_step].astype(jnp.bfloat16),
            "lat",
            split_axis=2,
            concat_axis=1,
            tiled=True,
        ).astype(jnp.float32)
        back_rows_list.append(
            lax.all_to_all(
                as_sent(adjoint_local(back_spec, *tables)),
                "lat",
                split_axis=1,
                concat_axis=2,
                tiled=True,
            )
        )
    grad_pieces = []
    for micro_step in range(MB):
        mats = mats_list[micro_step]
        grad_list, bias_parts = partial_grads[micro_step]
        back_enc = jnp.einsum(
            "grkc,ik->gric", back_rows_list[micro_step], analysis, precision=high
        ).reshape(columns, C)
        enc_low = back_enc.astype(jnp.bfloat16)
        grad_list[0] = weight_grad(rows_list[micro_step], enc_low)
        bias_parts[0] = jnp.sum(back_enc, axis=0)
        input_grad = back_enc + back_prod(enc_low, mats[0])
        grad_pieces.append(input_grad.reshape(globes, row_count, NLON, C))
        flat_grad = jnp.concatenate([member.reshape(-1) for member in grad_list])
        bias_total = bias_total + jnp.concatenate(bias_parts)
        mat_total = mat_total + lax.psum_scatter(
            flat_grad, ("dp", "lat"), scatter_dimension=0, tiled=True
        )
    bias_sum, square_sum = lax.psum((bias_total, jnp.sum(mat_total * mat_total)), ("dp", "lat"))
    grad_norm = jnp.sqrt(square_sum + jnp.sum(bias_sum * bias_sum))
    clip_factor = jnp.minimum(1.0, clip_norm / (grad_norm + 1e-06))
    mat_grad = mat_total * clip_factor
    bias_grad = bias_sum * clip_factor
    steps_done = step_count[0].astype(jnp.float32)
    mat_new, mat_moment_new, mat_second_new = adam_update(
        mat_master, mat_moment, mat_second, mat_grad, steps_done
    )
    bias_new, bias_moment_new, bias_second_new = adam_update(
        bias_master, bias_moment, bias_second, bias_grad, steps_done
    )
    state_out = jnp.concatenate(state_pieces, axis=0)
    state_grad = jnp.concatenate(grad_pieces, axis=0)
    return (
        state_out,
        state_grad,
        mat_grad,
        mat_new,
        mat_new.astype(jnp.bfloat16),
        mat_moment_new,
        mat_second_new,
        bias_grad,
        bias_new,
        bias_moment_new,
        bias_second_new,
        grad_norm.reshape(1),
    )


def solution(mesh):
    return jax.shard_map(
        local,
        mesh=mesh,
        in_specs=(
            P("dp", "lat", None, None),
            P("dp", "lat", None, None),
            P("dp", "lat", None, None),
            P(("dp", "lat")),
            P(("dp", "lat")),
            P(("dp", "lat")),
            P(),
            P(),
            P(),
            P(),
            P(),
            P(),
        ),
        out_specs=(
            P("dp", "lat", None, None),
            P("dp", "lat", None, None),
            P(("dp", "lat")),
            P(("dp", "lat")),
            P(("dp", "lat")),
            P(("dp", "lat")),
            P(("dp", "lat")),
            P(),
            P(),
            P(),
            P(),
            P(),
        ),
        check_vma=False,
    )
```

profile of v0, /device:TPU:1, one launch (start us, length us, event | category | flops | bytes accessed | tf_op | source)
XLA Modules:
  0.0 1027.4 jit_solution(16796806770152349891)
XLA Ops:
  10.6 77.9 %all-gather = bf16[256,1,1280]{2,1,0:T(2,128)(2,1)} all-gather(bf16[1,1,1280]{2,1,0:T(2,128)(2,1)S(1)} %reshape.944), channel_id=1, replica_groups=mesh['dp'=4,'lat'=64] {'dp','lat'}, dimensions={0}, use_global_device_ids=true | all-gather | bytes 657920 | tf_op jit(solution)/shard_map/all_gather | solution.py:200
  88.5 5.9 reduce.12
  99.9 6.6 all-to-all-start
  109.0 174.3 %while.19 = (s32[]{:T(128)}, f32[2,128]{1,0:T(2,128)S(1)}, f32[2,128]{1,0:T(2,128)S(1)}, f32[127,2,128]{2,0,1:T(8,128)S(1)}, f32[127]{0:T(128)S(1)}, /*index=5*/f32[128]{0:T(128)S(1)}, s32[]{:T(128)}, s32[]{:T(128)}, s32[]{:T(128)}) while((s32[]{:T(128)}, f32[2,128]{1,0:T(2,128)S(1)}, f32[2,128]{1,0:T(2,128)S(1)}, ...), condition=%wide.region_2.3_spmd.clone.clone, body=%wide.region_1.2_spmd.clone.clone.sunk | while | flops 1070 | bytes 9885 | solution.py:74
  297.5 10.5 %all-to-all-start.2 = ((bf16[2,2,256,128]{3,1,0,2:T(2,128)(2,1)}), bf16[2,2,256,128]{3,1,0,2:T(2,128)(2,1)}, u32[]{:S(2)}, u32[]{:S(2)}) async-start(bf16[2,2,256,128]{3,1,0,2:T(2,128)(2,1)} %copy.431), calls=%async_computation.2 | async-start | bytes 524288 | tf_op jit(solution)/shard_map/all_to_all | solution.py:220
  308.0 2.6 fusion.375
  312.2 8.9 all-to-all-done.2
  321.1 5.2 all-to-all-start.6
  340.3 11.0 %all-to-all-start.4 = ((bf16[2,2,256,128]{3,1,0,2:T(2,128)(2,1)}), bf16[2,2,256,128]{3,1,0,2:T(2,128)(2,1)}, u32[]{:S(2)}, u32[]{:S(2)}) async-start(bf16[2,2,256,128]{3,1,0,2:T(2,128)(2,1)} %copy.441), calls=%async_computation.4 | async-start | bytes 524288 | tf_op jit(solution)/shard_map/all_to_all | solution.py:220
  358.6 5.6 all-to-all-done.4
  372.2 5.1 all-to-all-start.5
  379.5 2.4 fusion.42
  391.9 11.2 %all-to-all-start.7 = ((bf16[2,128,4,128]{3,2,0,1:T(4,128)(2,1)}), bf16[2,128,4,128]{3,2,0,1:T(4,128)(2,1)}, u32[]{:S(2)}, u32[]{:S(2)}) async-start(bf16[2,128,4,128]{3,2,0,1:T(4,128)(2,1)} %copy.457), calls=%async_computation.7 | async-start | bytes 524288 | tf_op jit(solution)/shard_map/all_to_all | solution.py:228
  419.2 10.8 %all-to-all-start.1 = ((bf16[2,128,4,128]{3,2,0,1:T(4,128)(2,1)}), bf16[2,128,4,128]{3,2,0,1:T(4,128)(2,1)}, u32[]{:S(2)}, u32[]{:S(2)}) async-start(bf16[2,128,4,128]{3,2,0,1:T(4,128)(2,1)} %copy.427), calls=%async_computation.1 | async-start | bytes 524288 | tf_op jit(solution)/shard_map/all_to_all | solution.py:228
  446.2 10.9 %all-to-all-start.3 = ((bf16[2,128,4,128]{3,2,0,1:T(4,128)(2,1)}), bf16[2,128,4,128]{3,2,0,1:T(4,128)(2,1)}, u32[]{:S(2)}, u32[]{:S(2)}) async-start(bf16[2,128,4,128]{3,2,0,1:T(4,128)(2,1)} %copy.437), calls=%async_computation.3 | async-start | bytes 524288 | tf_op jit(solution)/shard_map/all_to_all | solution.py:228
  498.4 10.5 %all-to-all-start.12 = ((bf16[2,2,256,128]{3,1,0,2:T(2,128)(2,1)}), bf16[2,2,256,128]{3,1,0,2:T(2,128)(2,1)}, u32[]{:S(2)}, u32[]{:S(2)}) async-start(bf16[2,2,256,128]{3,1,0,2:T(2,128)(2,1)} %copy.481), calls=%async_computation.12 | async-start | bytes 524288 | tf_op jit(solution)/shard_map/all_to_all | solution.py:290
  532.1 10.5 %all-to-all-start.14 = ((bf16[2,2,256,128]{3,1,0,2:T(2,128)(2,1)}), bf16[2,2,256,128]{3,1,0,2:T(2,128)(2,1)}, u32[]{:S(2)}, u32[]{:S(2)}) async-start(bf16[2,2,256,128]{3,1,0,2:T(2,128)(2,1)} %copy.491), calls=%async_computation.14 | async-start | bytes 524288 | tf_op jit(solution)/shard_map/all_to_all | solution.py:290
  549.8 5.9 all-to-all-done.14
  555.7 5.2 all-to-all-start.8
  564.5 9.4 all-to-all-done.8
  574.6 5.1 all-to-all-start.10
  584.6 8.3 all-to-all-done.10
  592.9 5.1 all-to-all-start.13
  606.3 4.9 all-to-all-done.13
  611.2 5.8 all-to-all-start.15
  625.0 5.1 all-to-all-done.15
  630.1 5.4 all-to-all-start.9
  639.5 9.2 all-to-all-done.9
  648.7 5.1 all-to-all-start.11
  657.1 9.9 all-to-all-done.11
  687.5 247.0 %all-reduce.4.cloned.1.call-done = f32[327680]{0:T(1024)} async-done(((f32[327680]{0:T(1024)}), f32[327680]{0:T(1024)}) %all-reduce.4.cloned.1.call-update) | async-done | bytes 1310736
  937.4 77.7 %all-reduce.1 = (f32[]{:T(128)}, f32[1408]{0:T(1024)S(1)}) all-reduce(f32[]{:T(128)} %multiply_reduce_fusion.1, f32[1408]{0:T(1024)S(1)} %add_add_fusion.1), channel_id=1, replica_groups=mesh['dp'=4,'lat'=64] {'dp','lat'}, use_global_device_ids=true, to_apply=%region_8.9 | all-reduce | flops 1409 | bytes 11272 | tf_op jit(solution)/shard_map/psum | solution.py:323
  (1476 shorter events, 399.9 us)
Async XLA Ops:
  7.2 331.7 %copy-start = (f32[128,128]{1,0:T(8,128)S(1)}, f32[128,128]{1,0:T(8,128)}, u32[]{:S(2)}) copy-start(f32[128,128]{1,0:T(8,128)} %param.23) | copy-start | bytes 196612
  96.3 214.3 %copy-start.8 = (bf16[327680]{0:T(1024)(128)(2,1)}, bf16[327680]{0:T(1024)(128)(2,1)S(1)}, u32[]{:S(2)}) copy-start(bf16[327680]{0:T(1024)(128)(2,1)S(1)} %reshape.945) | copy-start | bytes 1966084
  99.9 197.6 %all-to-all-start = ((bf16[2,2,256,128]{3,1,0,2:T(2,128)(2,1)}), bf16[2,2,256,128]{3,1,0,2:T(2,128)(2,1)}, u32[]{:S(2)}, u32[]{:S(2)}) async-start(bf16[2,2,256,128]{3,1,0,2:T(2,128)(2,1)} %copy.420), calls=%async_computation | async-start | bytes 524288 | tf_op jit(solution)/shard_map/all_to_all | solution.py:220
  297.5 14.7 %copy-start.21 = (bf16[1024,128]{1,0:T(8,128)(2,1)}, bf16[1024,128]{1,0:T(8,128)(2,1)S(1)}, u32[]{:S(2)}) copy-start(bf16[1024,128]{1,0:T(8,128)(2,1)S(1)} %get-tuple-element.293) | copy-start | bytes 786436
  297.5 14.7 %copy-start.23 = (bf16[1024,128]{1,0:T(8,128)(2,1)}, bf16[1024,128]{1,0:T(8,128)(2,1)S(1)}, u32[]{:S(2)}) copy-start(bf16[1024,128]{1,0:T(8,128)(2,1)S(1)} %get-tuple-element.292) | copy-start | bytes 786436
  297.5 23.6 %all-to-all-start.2 = ((bf16[2,2,256,128]{3,1,0,2:T(2,128)(2,1)}), bf16[2,2,256,128]{3,1,0,2:T(2,128)(2,1)}, u32[]{:S(2)}, u32[]{:S(2)}) async-start(bf16[2,2,256,128]{3,1,0,2:T(2,128)(2,1)} %copy.431), calls=%async_computation.2 | async-start | bytes 524288 | tf_op jit(solution)/shard_map/all_to_all | solution.py:220
  321.1 19.3 %all-to-all-start.6 = ((bf16[2,2,256,128]{3,1,0,2:T(2,128)(2,1)}), bf16[2,2,256,128]{3,1,0,2:T(2,128)(2,1)}, u32[]{:S(2)}, u32[]{:S(2)}) async-start(bf16[2,2,256,128]{3,1,0,2:T(2,128)(2,1)} %copy.451), calls=%async_computation.6 | async-start | bytes 524288 | tf_op jit(solution)/shard_map/all_to_all | solution.py:220
  328.2 310.0 %copy-start.7 = (f32[256,256]{0,1:T(8,128)}, f32[256,256]{0,1:T(8,128)S(1)}, u32[]{:S(2)}) copy-start(f32[256,256]{0,1:T(8,128)S(1)} %reshape.870) | copy-start | bytes 786436
  340.3 23.9 %all-to-all-start.4 = ((bf16[2,2,256,128]{3,1,0,2:T(2,128)(2,1)}), bf16[2,2,256,128]{3,1,0,2:T(2,128)(2,1)}, u32[]{:S(2)}, u32[]{:S(2)}) async-start(bf16[2,2,256,128]{3,1,0,2:T(2,128)(2,1)} %copy.441), calls=%async_computation.4 | async-start | bytes 524288 | tf_op jit(solution)/shard_map/all_to_all | solution.py:220
  372.2 19.7 %all-to-all-start.5 = ((bf16[2,128,4,128]{3,2,0,1:T(4,128)(2,1)}), bf16[2,128,4,128]{3,2,0,1:T(4,128)(2,1)}, u32[]{:S(2)}, u32[]{:S(2)}) async-start(bf16[2,128,4,128]{3,2,0,1:T(4,128)(2,1)} %copy.447), calls=%async_computation.5 | async-start | bytes 524288 | tf_op jit(solution)/shard_map/all_to_all | solution.py:228
  391.9 27.3 %all-to-all-start.7 = ((bf16[2,128,4,128]{3,2,0,1:T(4,128)(2,1)}), bf16[2,128,4,128]{3,2,0,1:T(4,128)(2,1)}, u32[]{:S(2)}, u32[]{:S(2)}) async-start(bf16[2,128,4,128]{3,2,0,1:T(4,128)(2,1)} %copy.457), calls=%async_computation.7 | async-start | bytes 524288 | tf_op jit(solution)/shard_map/all_to_all | solution.py:228
  419.2 27.0 %all-to-all-start.1 = ((bf16[2,128,4,128]{3,2,0,1:T(4,128)(2,1)}), bf16[2,128,4,128]{3,2,0,1:T(4,128)(2,1)}, u32[]{:S(2)}, u32[]{:S(2)}) async-start(bf16[2,128,4,128]{3,2,0,1:T(4,128)(2,1)} %copy.427), calls=%async_computation.1 | async-start | bytes 524288 | tf_op jit(solution)/shard_map/all_to_all | solution.py:228
  446.2 31.5 %all-to-all-start.3 = ((bf16[2,128,4,128]{3,2,0,1:T(4,128)(2,1)}), bf16[2,128,4,128]{3,2,0,1:T(4,128)(2,1)}, u32[]{:S(2)}, u32[]{:S(2)}) async-start(bf16[2,128,4,128]{3,2,0,1:T(4,128)(2,1)} %copy.437), calls=%async_computation.3 | async-start | bytes 524288 | tf_op jit(solution)/shard_map/all_to_all | solution.py:228
  482.7 12.7 %copy-start.199 = (f32[1024,256]{1,0:T(8,128)}, f32[1024,256]{1,0:T(8,128)S(1)}, u32[]{:S(2)}) copy-start(f32[1024,256]{1,0:T(8,128)S(1)} %convolution_add_fusion.8) | copy-start | bytes 3145732
  498.4 33.7 %all-to-all-start.12 = ((bf16[2,2,256,128]{3,1,0,2:T(2,128)(2,1)}), bf16[2,2,256,128]{3,1,0,2:T(2,128)(2,1)}, u32[]{:S(2)}, u32[]{:S(2)}) async-start(bf16[2,2,256,128]{3,1,0,2:T(2,128)(2,1)} %copy.481), calls=%async_computation.12 | async-start | bytes 524288 | tf_op jit(solution)/shard_map/all_to_all | solution.py:290
  532.1 23.6 %all-to-all-start.14 = ((bf16[2,2,256,128]{3,1,0,2:T(2,128)(2,1)}), bf16[2,2,256,128]{3,1,0,2:T(2,128)(2,1)}, u32[]{:S(2)}, u32[]{:S(2)}) async-start(bf16[2,2,256,128]{3,1,0,2:T(2,128)(2,1)} %copy.491), calls=%async_computation.14 | async-start | bytes 524288 | tf_op jit(solution)/shard_map/all_to_all | solution.py:290
  555.7 18.3 %all-to-all-start.8 = ((bf16[2,2,256,128]{3,1,0,2:T(2,128)(2,1)}), bf16[2,2,256,128]{3,1,0,2:T(2,128)(2,1)S(1)}, u32[]{:S(2)}, u32[]{:S(2)}) async-start(bf16[2,2,256,128]{3,1,0,2:T(2,128)(2,1)} %copy.461), calls=%async_computation.8 | async-start | bytes 524288 | tf_op jit(solution)/shard_map/all_to_all | solution.py:290
  562.5 17.2 %copy-start.133 = (f32[128]{0:T(128)S(1)}, f32[128]{0:T(128)}, u32[]{:S(2)}) copy-start(f32[128]{0:T(128)} %get-tuple-element.242) | copy-start | bytes 1540
  574.6 18.3 %all-to-all-start.10 = ((bf16[2,2,256,128]{3,1,0,2:T(2,128)(2,1)}), bf16[2,2,256,128]{3,1,0,2:T(2,128)(2,1)}, u32[]{:S(2)}, u32[]{:S(2)}) async-start(bf16[2,2,256,128]{3,1,0,2:T(2,128)(2,1)} %copy.471), calls=%async_computation.10 | async-start | bytes 524288 | tf_op jit(solution)/shard_map/all_to_all | solution.py:290
  592.9 18.3 %all-to-all-start.13 = ((bf16[2,128,4,128]{3,2,0,1:T(4,128)(2,1)}), bf16[2,128,4,128]{3,2,0,1:T(4,128)(2,1)}, u32[]{:S(2)}, u32[]{:S(2)}) async-start(bf16[2,128,4,128]{3,2,0,1:T(4,128)(2,1)} %copy.487), calls=%async_computation.13 | async-start | bytes 524288 | tf_op jit(solution)/shard_map/all_to_all | solution.py:298
  606.3 15.2 %copy-start.45 = (f32[2,2,128,2,128]{2,4,3,0,1:T(8,128)S(1)}, f32[2,2,128,2,128]{2,4,3,0,1:T(8,128)}, u32[]{:S(2)}) copy-start(f32[2,2,128,2,128]{2,4,3,0,1:T(8,128)} %fusion.19) | copy-start | bytes 1572868
  611.2 18.9 %all-to-all-start.15 = ((bf16[2,128,4,128]{3,2,0,1:T(4,128)(2,1)}), bf16[2,128,4,128]{3,2,0,1:T(4,128)(2,1)}, u32[]{:S(2)}, u32[]{:S(2)}) async-start(bf16[2,128,4,128]{3,2,0,1:T(4,128)(2,1)} %copy.497), calls=%async_computation.15 | async-start | bytes 524288 | tf_op jit(solution)/shard_map/all_to_all | solution.py:298
  630.1 18.6 %all-to-all-start.9 = ((bf16[2,128,4,128]{3,2,0,1:T(4,128)(2,1)}), bf16[2,128,4,128]{3,2,0,1:T(4,128)(2,1)S(1)}, u32[]{:S(2)}, u32[]{:S(2)}) async-start(bf16[2,128,4,128]{3,2,0,1:T(4,128)(2,1)} %copy.467), calls=%async_computation.9 | async-start | bytes 524288 | tf_op jit(solution)/shard_map/all_to_all | solution.py:298
  638.6 18.0 %copy-start.2 = (f32[256,2,2,128]{3,0,2,1:T(8,128)}, f32[256,2,2,128]{3,0,2,1:T(8,128)S(1)}, u32[]{:S(2)}) copy-start(f32[256,2,2,128]{3,0,2,1:T(8,128)S(1)} %fusion.165) | copy-start | bytes 1572868
  648.7 18.3 %all-to-all-start.11 = ((bf16[2,128,4,128]{3,2,0,1:T(4,128)(2,1)}), bf16[2,128,4,128]{3,2,0,1:T(4,128)(2,1)}, u32[]{:S(2)}, u32[]{:S(2)}) async-start(bf16[2,128,4,128]{3,2,0,1:T(4,128)(2,1)} %copy.477), calls=%async_computation.11 | async-start | bytes 524288 | tf_op jit(solution)/shard_map/all_to_all | solution.py:298
  653.8 280.8 %all-reduce.4.cloned.1.call-start = ((), (), s32[]{:S(2)}) async-start(), calls=%async_computation.16 | async-start | bytes 2621440
  935.9 81.2 %copy-start.140 = (f32[1408]{0:T(1024)S(1)}, f32[1408]{0:T(1024)}, u32[]{:S(2)}) copy-start(f32[1408]{0:T(1024)} %param.20) | copy-start | bytes 16900
  935.9 81.2 %copy-start.149 = (f32[1408]{0:T(1024)S(1)}, f32[1408]{0:T(1024)}, u32[]{:S(2)}) copy-start(f32[1408]{0:T(1024)} %param.22) | copy-start | bytes 16900
  935.9 81.2 %copy-start.150 = (f32[1408]{0:T(1024)S(1)}, f32[1408]{0:T(1024)}, u32[]{:S(2)}) copy-start(f32[1408]{0:T(1024)} %param.21) | copy-start | bytes 16900
  935.9 81.9 %copy-start.134 = (f32[1280]{0:T(1024)S(1)}, f32[1280]{0:T(1024)}, u32[]{:S(2)}) copy-start(f32[1280]{0:T(1024)} %param.17) | copy-start | bytes 15364
  935.9 81.9 %copy-start.143 = (f32[1280]{0:T(1024)S(1)}, f32[1280]{0:T(1024)}, u32[]{:S(2)}) copy-start(f32[1280]{0:T(1024)} %param.19) | copy-start | bytes 15364
  935.9 81.9 %copy-start.144 = (f32[1280]{0:T(1024)S(1)}, f32[1280]{0:T(1024)}, u32[]{:S(2)}) copy-start(f32[1280]{0:T(1024)} %param.18) | copy-start | bytes 15364
  (188 other events, 355.3 us)
Sparse Core Ops, SparseCore 0:
  683.8 250.6 all-reduce.3
where the time goes:
time: 1040 us; the launch traced here: 1030 us
  waiting for transfers between devices  314 us (30%)
  local copies, waits for them, and re-layouts  176 us (17%)
  blocking collectives  156 us (15%)
  starting transfers between devices  124 us (12%)
  matrix products  118 us (11%)
  other arithmetic  117 us (11%)
  between operations  20.3 us (2%)
    unnamed x2, waiting for transfers between devices  247 us
    sqrt x127, other arithmetic, advance(): jnp.sqrt(jnp.maximum((degree_less * degree_less - wavenumber * wavenumber...  84.6 us
    all_gather x1, blocking collectives, local(): gathered = lax.all_gather(master_low, ('dp', 'lat'), axis=0, tiled=True)  77.9 us
    psum x1, blocking collectives, local(): lax.psum((bias_total, jnp.sum(mat_total * mat_total)), ('dp', 'lat'))  77.7 us
    dynamic_slice x127, local copies, waits for them, and re-layouts, legendre_table(): lax.scan(advance, (initial, jnp.zeros_like(initial)), offsets)  74.5 us
    dot_general x28, matrix products, back_prod(): lax.dot_general(grads_low, matrix, (((1,), (1,)), ((), ())), preferred_el...  39 us
    unnamed x466, local copies, waits for them, and re-layouts  38.4 us
    all_to_all x4, starting transfers between devices, local(): lax.all_to_all(as_sent(dynamics_local(spec_in, *tables)), 'lat', split_ax...  38 us
  transfers between devices with their start and end apart: 17, of which 10 were waited for; matrix products, arithmetic and copies ran while one was open for 33% of the time, Pallas kernels for 0%

commit v1 on v0

v1 whole, which is shorter than its diff:
```python
import functools
import math

import jax
import jax.numpy as jnp
import ml_dtypes
import numpy as np
from jax import lax
from jax.experimental import pallas as pl
from jax.experimental.pallas import tpu as pltpu
from jax.sharding import PartitionSpec as P

C = 128
F = 128
H = 256
NLAT = 128
NLON = 256
MW = 128
CH = 4
LATS = 64
XS = 4
BIAS_ROWS = 11

beta_one = 0.9
beta_two = 0.95
learn_rate = 0.3
decay_rate = 0.1
adam_eps = 1e-08
clip_norm = 1.0

MESH = pl.DeviceIdType.MESH
f32 = jnp.float32
bf16 = jnp.bfloat16


def zonal_tables():
    wave = np.arange(MW)
    turns = wave[:, None] * np.arange(NLON)[None, :] % NLON
    angle = turns * (2.0 * np.pi / NLON)
    rows = np.stack([np.cos(angle), -np.sin(angle)], axis=1).reshape(2 * MW, NLON)
    swapped = rows.reshape(MW // 4, 2, 4, NLON)[:, ::-1].reshape(2 * MW, NLON)
    both = np.stack([rows, swapped])
    turned = np.swapaxes(both, 1, 2)
    return both.astype(ml_dtypes.bfloat16), turned.astype(ml_dtypes.bfloat16)


def dot(left, right):
    return jnp.dot(left, right, preferred_element_type=f32)


def dot_nt(left, right):
    return lax.dot_general(left, right, (((1,), (1,)), ((), ())), preferred_element_type=f32)


def dot_tn(left, right):
    return lax.dot_general(left, right, (((0,), (0,)), ((), ())), preferred_element_type=f32)


def halves(value):
    top = value.astype(bf16)
    return top, (value - top.astype(f32)).astype(bf16)


def kernel(
    x_hbm,
    frc_hbm,
    cot_hbm,
    wsh_hbm,
    small_hbm,
    lc_hbm,
    bk_hbm,
    bi_hbm,
    so_hbm,
    sg_hbm,
    blk_hbm,
    fin_hbm,
    xv,
    fv,
    cv,
    ov,
    gv,
    wsh,
    small,
    lc,
    bk,
    bi,
    s1,
    r1,
    s2,
    r2,
    s3,
    r3,
    s4,
    r4,
    lq,
    lp,
    lqt,
    lpt,
    cx,
    pex,
    fac,
    fil,
    kap,
    qs,
    wg,
    wflat,
    we,
    ww,
    w5,
    wd,
    lch,
    ff,
    hid,
    gel,
    dwe,
    dww,
    dw5,
    dwd,
    db,
    gf,
    rx,
    s1r,
    rp,
    s2r,
    rq,
    blk,
    pps,
    ppr,
    px,
    pxr,
    pz,
    pzr,
    tot,
    pgr,
    fin,
    xsem,
    isem,
    osem,
    ssem,
    rsem,
    gs,
    gr,
):
    xme = lax.axis_index("dp")
    me = lax.axis_index("lat")
    zme = lax.div(me, 8)
    bme = lax.rem(me, 8)
    odd = lax.rem(me, 2)

    def x_copy(ch):
        part = pl.ds(2 * ch, 2)
        return pltpu.make_async_copy(x_hbm.at[part], xv.at[part], xsem.at[ch])

    loads = [
        pltpu.make_async_copy(bk_hbm, bk, isem.at[0]),
        pltpu.make_async_copy(wsh_hbm, wsh, isem.at[1]),
        pltpu.make_async_copy(small_hbm, small, isem.at[2]),
        pltpu.make_async_copy(lc_hbm, lc, isem.at[3]),
        pltpu.make_async_copy(bi_hbm, bi, isem.at[4]),
        pltpu.make_async_copy(frc_hbm, fv, isem.at[5]),
        pltpu.make_async_copy(cot_hbm, cv, isem.at[6]),
    ]
    loads[0].start()
    for ch in range(CH):
        x_copy(ch).start()
    for load in loads[1:]:
        load.start()

    barrier = pltpu.get_barrier_semaphore()

    def greet(step, carry):
        pl.semaphore_signal(
            barrier, inc=1, device_id={"lat": lax.rem(me + step, LATS)}, device_id_type=MESH
        )
        return carry

    lax.fori_loop(1, LATS, greet, 0)
    for step in range(1, XS):
        pl.semaphore_signal(
            barrier, inc=1, device_id={"dp": lax.rem(xme + step, XS)}, device_id_type=MESH
        )

    sub8 = lax.broadcasted_iota(jnp.int32, (LATS // 2, 8, 128), 1)
    lower = sub8 < 4

    def lat_copy(src, dst, send, recv, peer):
        return pltpu.make_async_remote_copy(
            src_ref=src,
            dst_ref=dst,
            send_sem=send,
            recv_sem=recv,
            device_id={"lat": peer},
            device_id_type=MESH,
        )

    def dp_copy(src, dst, send, recv, peer):
        return pltpu.make_async_remote_copy(
            src_ref=src,
            dst_ref=dst,
            send_sem=send,
            recv_sem=recv,
            device_id={"dp": peer},
            device_id_type=MESH,
        )

    def drain(ref, sem):
        pltpu.make_async_copy(ref, ref, sem).wait()

    def exchange(phase, src, dst, ch):
        def one(step, carry):
            peer = lax.rem(me + step, LATS)
            lat_copy(
                src.at[ch, peer], dst.at[ch, me], ssem.at[phase, ch], rsem.at[phase, ch], peer
            ).start()
            return carry

        lax.fori_loop(1, LATS, one, 0)
        dst[ch, me] = src[ch, me]

    def arrived(phase, dst, ch):
        drain(dst.at[ch, pl.ds(0, LATS - 1)], rsem.at[phase, ch])

    def to_plane(src_of, dst, number):
        for step in range(1, 8):
            other = lax.rem(bme + step, 8)
            lat_copy(src_of(other), dst, gs.at[number], gr.at[number], zme * 8 + other).start()

    def to_column(src, dst, number):
        for step in range(1, 8):
            other = lax.rem(zme + step, 8)
            lat_copy(src, dst, gs.at[number], gr.at[number], other * 8 + bme).start()

    def to_line(src_of, dst, number):
        for step in range(1, XS):
            other = lax.rem(xme + step, XS)
            dp_copy(src_of(other), dst, gs.at[number], gr.at[number], other).start()

    def pack(first, second):
        evens = []
        odds = []
        for globe in range(2):
            lanes = slice(globe * 128, globe * 128 + 128)
            plain = first[:, lanes].reshape(LATS // 2, 8, 128)
            turned = second[:, lanes].reshape(LATS // 2, 8, 128)
            evens.append(jnp.where(lower, plain, turned))
            odds.append(jnp.where(lower, turned, plain))
        even = jnp.concatenate(evens, axis=1).astype(bf16)
        other = jnp.concatenate(odds, axis=1).astype(bf16)
        return jnp.stack([even, other], axis=1).reshape(LATS, 16, 128)

    def unpack(tiles, row):
        pairs = tiles.astype(f32).reshape(LATS // 2, 2, 16, 128)
        straight = jnp.where(row == 0, 1, 0)
        pick = jnp.where(lower, 1, 0) == straight
        sides = []
        for globe in range(2):
            even = pairs[:, 0, globe * 8 : globe * 8 + 8]
            other = pairs[:, 1, globe * 8 : globe * 8 + 8]
            sides.append(jnp.where(pick, even, other).reshape(2 * MW, 128))
        return jnp.concatenate(sides, axis=1).astype(bf16)

    loads[0].wait()

    def analyse(ch, carry):
        x_copy(ch).wait()
        found = []
        for row in range(2):
            sides = jnp.concatenate([xv[2 * ch, row], xv[2 * ch + 1, row]], axis=1)
            found.append(dot(bk[row], sides.astype(bf16)))
        s1[ch] = pack(found[0], found[1])

        @pl.when(ch == 0)
        def _():
            loads[1].wait()
            wg[xme, zme, bme] = wsh[...]
            pl.semaphore_wait(barrier, LATS - 1 + XS - 1)
            to_column(wsh, wg.at[xme, zme, bme], 0)

        @pl.when(ch == 1)
        def _():
            drain(wg.at[0, pl.ds(0, 7), 0], gr.at[0])
            to_plane(lambda other: wg.at[xme, :, bme], wg.at[xme, :, bme], 1)

        @pl.when(ch == 2)
        def _():
            drain(wg.at[0, :, pl.ds(0, 7)], gr.at[1])
            to_line(lambda other: wg.at[xme], wg.at[xme], 2)

        exchange(0, s1, r1, ch)
        return carry

    lax.fori_loop(0, CH, analyse, 0)

    for load in loads[2:5]:
        load.wait()
    lane_col = lax.broadcasted_iota(jnp.int32, (128, 1024), 1)
    lat_index = lax.broadcasted_iota(jnp.int32, (128, 1024), 0)
    row_bit = lax.rem(lax.rem(lax.div(lane_col, 4), 2) + odd, 2)
    one_hot = jnp.where(lat_index == 2 * lax.div(lane_col, 16) + row_bit, 1.0, 0.0).astype(bf16)
    lat = dot(small[16:24, :].astype(bf16), one_hot)[0:1, :]
    phi = (lat + 0.5) * (math.pi / NLAT) - 0.5 * math.pi
    mu = jnp.sin(phi)
    cos_phi = jnp.cos(phi)

    sub = lax.broadcasted_iota(jnp.int32, (128, 128), 0)
    lane = lax.broadcasted_iota(jnp.int32, (128, 128), 1)
    m_zero = 2 * me
    k_safe = jnp.maximum(sub, 1).astype(f32)
    logs = jnp.log((2.0 * k_safe + 1.0) / (2.0 * k_safe))
    starts = []
    for slot in range(2):
        below = (sub >= 1) & (sub <= m_zero + slot)
        starts.append(
            -0.5 * math.log(2.0) + 0.5 * jnp.sum(jnp.where(below, logs, 0.0), axis=0, keepdims=True)
        )
    slot_lane = lax.rem(lax.div(lane, 2), 2)
    start = jnp.where(slot_lane[0:1] == 0, starts[0], starts[1])
    start = jnp.concatenate([start] * 8, axis=1)
    m_lane = (m_zero + slot_lane).astype(f32)
    m_wide = jnp.concatenate([m_lane[0:1]] * 8, axis=1)
    first = jnp.exp(start + m_wide * jnp.log(cos_phi))
    degree = m_lane + sub.astype(f32)
    less = degree - 1.0
    m_square = m_lane * m_lane
    gap = jnp.where(sub == 0, 1.0, degree * degree - m_square)
    fac[0] = jnp.sqrt(jnp.maximum((4.0 * degree * degree - 1.0) / gap, 0.0))
    fac[1] = jnp.sqrt(jnp.maximum((less * less - m_square) / (4.0 * less * less - 1.0), 0.0))
    pex[0:1, :] = first

    def advance(n, pair):
        latest, earlier = pair
        up = jnp.concatenate([fac[0, pl.ds(n, 1), :]] * 8, axis=1)
        down = jnp.concatenate([fac[1, pl.ds(n, 1), :]] * 8, axis=1)
        now = up * (mu * latest - down * earlier)
        pex[pl.ds(n, 1), :] = now
        return (now, latest)

    lax.fori_loop(1, MW, advance, (first, jnp.zeros_like(first)))

    for slot in range(2):
        deg = (m_zero + slot + sub).astype(f32)
        live = deg < MW - 0.5
        ratio = deg / MW
        ratio = ratio * ratio
        ratio = ratio * ratio
        fil[slot] = jnp.where(live, jnp.exp(-(ratio * ratio)), 0.0)
        kap[slot] = deg * (deg + 1.0) / (MW * (MW - 1.0))

    n_wide = lax.broadcasted_iota(jnp.int32, (128, 1024), 0)
    keep = n_wide.astype(f32) + m_wide < MW - 0.5
    weight = jnp.where(m_wide == 0.0, 1.0, 2.0)
    poly = jnp.where(keep, pex[...], 0.0)
    synth = poly * weight
    quad = poly * ((math.pi / NLAT) * cos_phi)
    anal = quad * (1.0 / NLON)
    synth_t = synth.T
    anal_t = anal.T
    lane16 = lax.rem(lane_col[0:1], 16)
    row16 = lax.rem(lax.broadcasted_iota(jnp.int32, (1024, 128), 0), 16)

    def chosen(sixteen, combo):
        return (
            (lax.div(sixteen, 8) == combo // 4)
            & (lax.rem(lax.div(sixteen, 2), 2) == (combo // 2) % 2)
            & (lax.rem(sixteen, 2) == combo % 2)
        )

    for combo in range(8):
        part = slice(combo * 128, combo * 128 + 128)
        mine = chosen(lane16, combo)
        lp[part, :] = jnp.where(mine, synth, 0.0).astype(bf16)
        lq[part, :] = jnp.where(mine, anal, 0.0).astype(bf16)
        mine_t = chosen(row16, combo)
        lpt[:, part] = jnp.where(mine_t, synth_t, 0.0).astype(bf16)
        lqt[:, part] = jnp.where(mine_t, anal_t, 0.0).astype(bf16)
    zero_wave = jnp.sum(jnp.where(chosen(lane16, 0), quad, 0.0), axis=1, keepdims=True)
    zero_wave = jnp.where(me == 0, zero_wave, 0.0)
    qs[...] = jnp.broadcast_to(zero_wave, (128, 128))
    lc_top, lc_low = halves(lc[...])
    lch[0] = lc_top
    lch[1] = lc_low

    drain(wg.at[pl.ds(0, 3)], gr.at[2])

    def spread(group, carry):
        tiles = wg[lax.div(group, 8), lax.rem(group, 8)].astype(f32)
        rows = wflat.at[pl.ds(pl.multiple_of(group * 80, 8), 80)]
        for b in range(8):
            rows[b * 10 : b * 10 + 10, :] = tiles[b, 0:10, :]
        return carry

    lax.fori_loop(0, 32, spread, 0)
    we[...] = wflat[0:128, :].astype(bf16)
    for layer in range(4):
        for side in range(2):
            begin = 128 + 512 * layer + side
            ww[layer, :, side * 128 : side * 128 + 128] = wflat[
                pl.ds(begin, 256, stride=2), :
            ].astype(bf16)
    w5[...] = wflat[2176:2432, :].astype(bf16)
    wd[...] = wflat[2432:2560, :].astype(bf16)
    dwe[...] = jnp.zeros_like(dwe)
    dww[...] = jnp.zeros_like(dww)
    dw5[...] = jnp.zeros_like(dw5)
    dwd[...] = jnp.zeros_like(dwd)
    db[...] = jnp.zeros_like(db)

    def couple(value, transposed):
        top, low = halves(value)
        product = dot_nt if transposed else dot
        return product(top, lch[0]) + product(top, lch[1]) + product(low, lch[0])

    def per_slot(table):
        both = jnp.concatenate([table[0], table[0], table[1], table[1]], axis=0)
        return jnp.concatenate([both, both], axis=0)

    zero_combos = (0, 4)

    def add_zero_wave(value, extra):
        blocks = [value[c * 128 : c * 128 + 128] for c in range(8)]
        for c in zero_combos:
            blocks[c] = blocks[c] + extra
        return jnp.concatenate(blocks, axis=0)

    def dynamics(ch, carry):
        arrived(0, r1, ch)
        coef = dot(lq[...], r1[ch].reshape(1024, 128))
        coef_low = coef.astype(bf16)
        cx[ch] = coef_low
        coef = coef + dot(coef_low, we[...])
        coef = add_zero_wave(coef, qs[...] * small[0:1, :])
        coef = per_slot(fil) * (coef - per_slot(kap) * couple(coef, False))
        s2[ch] = dot(lpt[...], coef.astype(bf16)).astype(bf16).reshape(LATS, 16, 128)
        exchange(1, s2, r2, ch)
        return carry

    lax.fori_loop(0, CH, dynamics, 0)

    loads[5].wait()
    loads[6].wait()
    out_copy = [
        lambda ch: pltpu.make_async_copy(
            ov.at[pl.ds(2 * ch, 2)], so_hbm.at[pl.ds(2 * ch, 2)], osem.at[0, ch]
        ),
        lambda ch: pltpu.make_async_copy(
            gv.at[pl.ds(2 * ch, 2)], sg_hbm.at[pl.ds(2 * ch, 2)], osem.at[1, ch]
        ),
    ]
    c_zero = math.sqrt(2.0 / math.pi)
    c_one = 0.044715

    def bias_row(index, count):
        return jnp.concatenate([small[index + k : index + k + 1, :] for k in range(count)], axis=1)

    def add_bias(index, value):
        total = jnp.sum(value, axis=0, keepdims=True)
        for k in range(value.shape[1] // 128):
            db[index + k : index + k + 1, :] += total[:, k * 128 : k * 128 + 128]

    def two(ref, ch, row):
        return jnp.concatenate([ref[2 * ch, row], ref[2 * ch + 1, row]], axis=0)

    def columns(ch):
        def block(row, carry):
            grid = dot(bi[row], unpack(r2[ch], row))
            dynamic = jnp.concatenate([grid[:, 0:128], grid[:, 128:256]], axis=0)
            hidden = jnp.concatenate([dynamic.astype(bf16), two(fv, ch, row)], axis=1)
            hid[0] = hidden
            for layer in range(4):
                pre = dot(hidden, ww[layer]) + bias_row(1 + 2 * layer, 2)
                square = pre * pre
                inner = pre * (c_zero + (c_zero * c_one) * square)
                bent = jnp.tanh(inner)
                half = 0.5 * pre
                hidden = (half + half * bent).astype(bf16)
                slope = half * (c_zero + (3.0 * c_zero * c_one) * square)
                gel[layer] = (0.5 + 0.5 * bent) + slope * (1.0 - bent * bent)
                hid[layer + 1] = hidden
            middle = dynamic + dot(hidden, w5[...]) + bias_row(9, 1)
            middle_low = middle.astype(bf16)
            output = middle + dot(middle_low, wd[...]) + bias_row(10, 1)
            ov[2 * ch, row] = output[0:256]
            ov[2 * ch + 1, row] = output[256:512]
            upstream = two(cv, ch, row)
            up_low = upstream.astype(bf16)
            dwd[...] += dot_tn(middle_low, up_low)
            add_bias(10, upstream)
            back_mid = upstream + dot_nt(up_low, wd[...])
            mid_low = back_mid.astype(bf16)
            dw5[...] += dot_tn(hidden, mid_low)
            add_bias(9, back_mid)
            back = dot_nt(mid_low, w5[...])
            for layer in (3, 2, 1, 0):
                back_pre = gel[layer] * back
                pre_low = back_pre.astype(bf16)
                dww[layer] += dot_tn(hid[layer], pre_low)
                add_bias(1 + 2 * layer, back_pre)
                if layer > 0:
                    back = dot_nt(pre_low, ww[layer])
                else:
                    back = dot_nt(pre_low, ww[0, 0:128, :])
            back_low = (back_mid + back).astype(bf16)
            sides = jnp.concatenate([back_low[0:256], back_low[256:512]], axis=1)
            ff[row] = dot(bk[row], sides)
            return carry

        lax.fori_loop(0, 2, block, 0)
        out_copy[0](ch).start()
        s3[ch] = pack(ff[0], ff[1])
        exchange(2, s3, r3, ch)

    def adjoint(ch):
        arrived(2, r3, ch)
        back = per_slot(fil) * dot(lp[...], r3[ch].reshape(1024, 128))
        back = back - couple(per_slot(kap) * back, True)
        back_low = back.astype(bf16)
        dwe[...] += dot_tn(cx[ch], back_low)
        flat = qs[...] * (back[0:128] + back[512:640])
        db[0:1, :] += jnp.sum(flat, axis=0, keepdims=True)
        back = back + dot_nt(back_low, we[...])
        s4[ch] = dot(lqt[...], back.astype(bf16)).astype(bf16).reshape(LATS, 16, 128)
        exchange(3, s4, r4, ch)

    def grad_line():
        gf[0:128, :] = jnp.zeros((128, 128), f32)
        for layer in range(4):
            for side in range(2):
                begin = 128 + 512 * layer + side
                gf[pl.ds(begin, 256, stride=2), :] = dww[layer, :, side * 128 : side * 128 + 128]
        gf[2176:2432, :] = dw5[...]
        gf[2432:2560, :] = dwd[...]
        to_line(lambda other: gf.at[pl.ds(pl.multiple_of(other * 640, 8), 640)], rx.at[xme], 3)

    def grad_plane():
        drain(rx.at[pl.ds(0, 3)], gr.at[3])
        total = gf[pl.ds(pl.multiple_of(xme * 640, 8), 640), :]
        for step in range(1, XS):
            total = total + rx[lax.rem(xme + step, XS)]
        s1r[...] = total
        to_plane(lambda other: s1r.at[pl.ds(pl.multiple_of(other * 80, 8), 80)], rp.at[bme], 4)

    def grad_turn():
        drain(rp.at[pl.ds(0, 7)], gr.at[4])
        total = s1r[pl.ds(pl.multiple_of(bme * 80, 8), 80), :]
        for step in range(1, 8):
            total = total + rp[lax.rem(bme + step, 8)]
        s2r[...] = total

        @pl.when(bme == zme)
        def _():
            rq[bme] = s2r[...]

        @pl.when(bme != zme)
        def _():
            lat_copy(s2r, rq.at[zme], gs.at[5], gr.at[5], bme * 8 + zme).start()

    def grad_share():
        @pl.when(bme != zme)
        def _():
            drain(s2r, gr.at[5])

        to_plane(lambda other: rq.at[bme], rq.at[bme], 6)

    def grad_block():
        drain(rq.at[pl.ds(0, 7)], gr.at[6])
        total = rq[0]
        for b in range(1, 8):
            total = total + rq[b]
        blk[...] = total

    def middle_steps(t, carry):
        @pl.when(t < CH)
        def _():
            arrived(1, r2, t)
            columns(t)

        @pl.when(t == CH - 1)
        def _():
            grad_line()

        @pl.when(t >= 2)
        def _():
            adjoint(t - 2)

        @pl.when(t == CH)
        def _():
            grad_plane()

        @pl.when(t == CH + 1)
        def _():
            grad_turn()

        return carry

    lax.fori_loop(0, CH + 2, middle_steps, 0)

    grad_share()
    for b in range(8):
        pps[b, 0:16, :] = dwe[b * 16 : b * 16 + 16, :]
        pps[b, 16:32, :] = db[...]
    to_plane(lambda other: pps.at[other], ppr.at[bme], 7)

    def last_line():
        grad_block()
        drain(ppr.at[pl.ds(0, 7)], gr.at[7])
        total = pps[bme]
        for step in range(1, 8):
            total = total + ppr[lax.rem(bme + step, 8)]
        px[0:32, :] = total
        square = blk[0:8, :] * blk[0:8, :]
        for k in range(1, 10):
            piece = blk[8 * k : 8 * k + 8, :]
            square = square + piece * piece
        px[32:40, :] = square
        to_line(lambda other: px, pxr.at[xme], 8)

    def last_column():
        drain(pxr.at[pl.ds(0, 3)], gr.at[8])
        total = px[...]
        for step in range(1, XS):
            total = total + pxr[lax.rem(xme + step, XS)]
        pz[...] = total
        to_column(pz, pzr.at[zme], 9)

    def last_plane():
        drain(pzr.at[pl.ds(0, 7)], gr.at[9])
        total = pz[...]
        for step in range(1, 8):
            total = total + pzr[lax.rem(zme + step, 8)]
        tot[...] = total
        pgr[bme] = tot[0:16, :]
        to_plane(lambda other: tot.at[pl.ds(0, 16)], pgr.at[bme], 10)

    def finish(ch, carry):
        @pl.when(ch == 1)
        def _():
            last_line()

        @pl.when(ch == 2)
        def _():
            last_column()

        @pl.when(ch == 3)
        def _():
            last_plane()

        arrived(3, r4, ch)
        for row in range(2):
            grid = dot(bi[row], unpack(r4[ch], row))
            gv[2 * ch, row] = grid[:, 0:128]
            gv[2 * ch + 1, row] = grid[:, 128:256]
        out_copy[1](ch).start()
        return carry

    lax.fori_loop(0, CH, finish, 0)

    drain(pgr.at[pl.ds(0, 7)], gr.at[10])
    enc = pgr[...].reshape(128, 128)
    at_zero = jnp.where((xme == 0) & (zme == 0), 1.0, 0.0)
    at_one = jnp.where((xme == 0) & (zme == 1), 1.0, 0.0)
    blk[...] += at_zero * enc[0:80]
    blk[0:48, :] += at_one * enc[80:128]
    bias_total = tot[16:32, :]
    squares = (
        jnp.sum(tot[32:40, :]) + jnp.sum(enc * enc) + jnp.sum(bias_total * bias_total)
    )
    fin[0:16, :] = bias_total
    fin[16:24, :] = jnp.zeros((8, 128), f32) + squares
    last = [
        pltpu.make_async_copy(blk, blk_hbm, isem.at[7]),
        pltpu.make_async_copy(fin, fin_hbm, isem.at[8]),
    ]
    for copy in last:
        copy.start()

    for phase, src in enumerate((s1, s2, s3, s4)):
        for ch in range(CH):
            drain(src.at[ch, pl.ds(0, LATS - 1)], ssem.at[phase, ch])
    drain(wg.at[0, pl.ds(0, 7), 0], gs.at[0])
    drain(wg.at[0, :, pl.ds(0, 7)], gs.at[1])
    drain(wg.at[pl.ds(0, 3)], gs.at[2])
    drain(rx.at[pl.ds(0, 3)], gs.at[3])
    drain(rp.at[pl.ds(0, 7)], gs.at[4])

    @pl.when(bme != zme)
    def _():
        drain(s2r, gs.at[5])

    drain(rq.at[pl.ds(0, 7)], gs.at[6])
    drain(ppr.at[pl.ds(0, 7)], gs.at[7])
    drain(pxr.at[pl.ds(0, 3)], gs.at[8])
    drain(pzr.at[pl.ds(0, 7)], gs.at[9])
    drain(pgr.at[pl.ds(0, 7)], gs.at[10])
    for ch in range(CH):
        out_copy[0](ch).wait()
        out_copy[1](ch).wait()
    for copy in last:
        copy.wait()


def adam_update(weights, moment, second, grads, steps_done):
    moment_new = beta_one * moment + (1.0 - beta_one) * grads
    second_new = beta_two * second + (1.0 - beta_two) * grads * grads
    moment_hat = moment_new / (1.0 - beta_one**steps_done)
    second_hat = second_new / (1.0 - beta_two**steps_done)
    weights_new = weights - learn_rate * (
        moment_hat / (jnp.sqrt(second_hat) + adam_eps) + decay_rate * weights
    )
    return (weights_new, moment_new, second_new)


def local(
    state,
    forcing,
    state_cot,
    mat_master,
    mat_moment,
    mat_second,
    bias_master,
    bias_moment,
    bias_second,
    level_coupling,
    lat_of_row,
    step_count,
):
    wsh = jnp.pad(mat_master.reshape(10, 128), ((0, 6), (0, 0))).astype(bf16)
    small = jnp.concatenate(
        [
            jnp.pad(bias_master.reshape(BIAS_ROWS, 128), ((0, 5), (0, 0))),
            jnp.broadcast_to(lat_of_row.astype(f32)[None, :], (8, 128)),
        ],
        axis=0,
    )
    both, turned = zonal_tables()
    any_spec = pl.BlockSpec(memory_space=pl.ANY)
    big = (8, 2, NLON, C)
    tiles = (CH, LATS, 16, 128)
    vm = pltpu.VMEM
    scratch = [
        vm(big, f32),
        vm(big, bf16),
        vm(big, f32),
        vm(big, f32),
        vm(big, f32),
        vm((16, 128), bf16),
        vm((24, 128), f32),
        vm((128, 128), f32),
        vm((2, 256, 256), bf16),
        vm((2, 256, 256), bf16),
        *[vm(tiles, bf16) for _ in range(8)],
        *[vm((1024, 1024), bf16) for _ in range(4)],
        vm((CH, 1024, 128), bf16),
        vm((128, 1024), f32),
        vm((2, 128, 128), f32),
        vm((2, 128, 128), f32),
        vm((2, 128, 128), f32),
        vm((128, 128), f32),
        vm((XS, 8, 8, 16, 128), bf16),
        vm((2560, 128), f32),
        vm((128, 128), bf16),
        vm((4, 256, 256), bf16),
        vm((256, 128), bf16),
        vm((128, 128), bf16),
        vm((2, 128, 128), bf16),
        vm((2, 256, 256), f32),
        vm((5, 512, 256), bf16),
        vm((4, 512, 256), f32),
        vm((128, 128), f32),
        vm((4, 256, 256), f32),
        vm((256, 128), f32),
        vm((128, 128), f32),
        vm((16, 128), f32),
        vm((2560, 128), f32),
        vm((XS, 640, 128), f32),
        vm((640, 128), f32),
        vm((8, 80, 128), f32),
        vm((80, 128), f32),
        vm((8, 80, 128), f32),
        vm((80, 128), f32),
        vm((8, 32, 128), f32),
        vm((8, 32, 128), f32),
        vm((40, 128), f32),
        vm((XS, 40, 128), f32),
        vm((40, 128), f32),
        vm((8, 40, 128), f32),
        vm((40, 128), f32),
        vm((8, 16, 128), f32),
        vm((24, 128), f32),
        pltpu.SemaphoreType.DMA((CH,)),
        pltpu.SemaphoreType.DMA((9,)),
        pltpu.SemaphoreType.DMA((2, CH)),
        pltpu.SemaphoreType.DMA((4, CH)),
        pltpu.SemaphoreType.DMA((4, CH)),
        pltpu.SemaphoreType.DMA((11,)),
        pltpu.SemaphoreType.DMA((11,)),
    ]
    state_out, state_grad, block, final = pl.pallas_call(
        kernel,
        out_shape=(
            jax.ShapeDtypeStruct(big, f32),
            jax.ShapeDtypeStruct(big, f32),
            jax.ShapeDtypeStruct((80, 128), f32),
            jax.ShapeDtypeStruct((24, 128), f32),
        ),
        in_specs=[any_spec] * 8,
        out_specs=(any_spec,) * 4,
        scratch_shapes=scratch,
        compiler_params=pltpu.CompilerParams(
            collective_id=0, has_side_effects=True, vmem_limit_bytes=60 * 1024 * 1024
        ),
        cost_estimate=pl.CostEstimate(
            flops=16 * 10**9, bytes_accessed=10 * 2**20, transcendentals=4 * 10**6
        ),
        name="column_step",
    )(
        state,
        forcing,
        state_cot,
        wsh,
        small,
        level_coupling,
        jnp.asarray(both),
        jnp.asarray(turned),
    )

    bias_sum = final[0:BIAS_ROWS].reshape(-1)
    grad_norm = jnp.sqrt(final[16, 0])
    clip_factor = jnp.minimum(1.0, clip_norm / (grad_norm + 1e-06))
    place = lax.rem(lax.axis_index("lat"), 8) * 10
    mat_total = lax.dynamic_slice(block, (place, 0), (10, 128)).reshape(-1)
    mat_grad = mat_total * clip_factor
    bias_grad = bias_sum * clip_factor
    steps_done = step_count[0].astype(f32)
    mat_new, mat_moment_new, mat_second_new = adam_update(
        mat_master, mat_moment, mat_second, mat_grad, steps_done
    )
    bias_new, bias_moment_new, bias_second_new = adam_update(
        bias_master, bias_moment, bias_second, bias_grad, steps_done
    )
    return (
        state_out,
        state_grad,
        mat_grad,
        mat_new,
        mat_new.astype(bf16),
        mat_moment_new,
        mat_second_new,
        bias_grad,
        bias_new,
        bias_moment_new,
        bias_second_new,
        grad_norm.reshape(1),
    )


def solution(mesh):
    columns = P("dp", "lat", None, None)
    flat = P(("dp", "lat"))
    return jax.shard_map(
        local,
        mesh=mesh,
        in_specs=(columns,) * 3 + (flat,) * 3 + (P(),) * 6,
        out_specs=(columns,) * 2 + (flat,) * 5 + (P(),) * 5,
        check_vma=False,
    )
```

time: 1040 us -> 152 us (0.15); the launches traced: 1030 us -> 152 us
  waiting for transfers between devices: 314 us -> 0 us
  local copies, waits for them, and re-layouts: 176 us -> 6.4 us
  blocking collectives: 156 us -> 0 us
  Pallas kernels: 0 us -> 137 us
  starting transfers between devices: 124 us -> 0 us
  matrix products: 118 us -> 0 us
  other arithmetic: 117 us -> 5.34 us
  between operations: 20.3 us -> 3.31 us
    unnamed x2 -> x0, waiting for transfers between devices: 247 us -> none
    pallas_call x0 -> x1, Pallas kernels: none -> 137 us  [local(): pl.pallas_call(kernel, out_shape=(jax.ShapeDtypeStruct(big, f32), jax.Sha...]
    all_to_all x16 -> x0, starting transfers between devices: 124 us -> none  [the longest x4 38 us: local(): lax.all_to_all(as_sent(dynamics_local(spec_in, *tables)), 'lat', split_ax...]
    dot_general x124 -> x0, matrix products: 118 us -> none  [the longest x28 39 us: back_prod(): lax.dot_general(grads_low, matrix, (((1,), (1,)), ((), ())), preferred_el...]
    sqrt x127 -> x0, other arithmetic: 84.6 us -> none  [advance(): jnp.sqrt(jnp.maximum((degree_less * degree_less - wavenumber * wavenumber...]
    all_gather x1 -> x0, blocking collectives: 77.9 us -> none  [local(): gathered = lax.all_gather(master_low, ('dp', 'lat'), axis=0, tiled=True)]
    psum x1 -> x0, blocking collectives: 77.7 us -> none  [local(): lax.psum((bias_total, jnp.sum(mat_total * mat_total)), ('dp', 'lat'))]
    dynamic_slice x127 -> x0, local copies, waits for them, and re-layouts: 74.5 us -> none  [legendre_table(): lax.scan(advance, (initial, jnp.zeros_like(initial)), offsets)]
  transfers between devices with their start and end apart: 17 -> 0, of which waited for: 10 -> 0; matrix products, arithmetic and copies ran while one was open for 33% -> 0% of each run, Pallas kernels for 0% -> 0%
where the time goes in v1:
time: 152 us
  Pallas kernels  137 us (90%)
  local copies, waits for them, and re-layouts  6.4 us (4%)
  other arithmetic  5.34 us (4%)
  between operations  3.31 us (2%)
    pallas_call x1, Pallas kernels, local(): pl.pallas_call(kernel, out_shape=(jax.ShapeDtypeStruct(big, f32), jax.Sha...  137 us
    unnamed x16, local copies, waits for them, and re-layouts  4.61 us

profile of v1, /device:TPU:1, one launch (start us, length us, event | category | flops | bytes accessed | tf_op | source)
XLA Modules:
  0.0 151.6 jit_solution(13207599149633243062)
XLA Ops:
  0.6 0.7 convert_bitcast_fusion
  1.3 0.6 pad.9.wsh_hbm
  1.9 0.7 convert_element_type.15
  2.6 1.3 select_maximum_fusion.small_hbm
  3.9 0.0 copy-start.1
  3.9 0.0 copy-start.3
  3.9 0.0 copy-start.4
  3.9 0.0 copy-start.2
  3.9 0.0 copy-start.5
  3.9 0.0 copy-start.6
  3.9 136.5 %column_step.1 = (f32[8,2,256,128]{3,2,1,0:T(8,128)}, f32[8,2,256,128]{3,2,1,0:T(8,128)}, f32[80,128]{1,0:T(8,128)}, f32[24,128]{1,0:T(8,128)}) custom-call(f32[8,2,256,128]{3,2,1,0:T(8,128)} %x_hbm.1, bf16[8,2,256,128]{3,2,1,0:T(8,128)(2,1)} %frc_hbm.1, f32[8,2,256,128]{3,2,1,0:T(8,128)} %cot_hbm.1, bf16[16,128]{1,0:T(8,128)(2,1)} %pad.9.wsh_hbm, ...), custom_call_target="tpu_custom_call" | custom-call | flops 16000000000 | bytes 10485760 | tf_op jit(solution)/shard_map/column_step/pallas_call | solution.py:797
  141.2 1.2 slice.6
  143.1 0.0 copy-done.1
  143.1 0.0 copy-done.3
  143.2 0.0 copy-done.4
  143.2 1.4 fusion.3
  144.5 0.0 copy-done.2
  144.5 0.0 copy-done.5
  144.5 0.0 copy-done.6
  144.5 1.3 multiply_subtract_fusion
  145.9 0.0 copy-start
  145.9 3.3 %copy.29 = f32[8,2,256,128]{3,2,1,0:T(8,128)} copy(f32[8,2,256,128]{3,2,1,0:T(8,128)} %get-tuple-element.41) | data formatting | bytes 4194304
  149.1 0.0 copy-done
  149.1 1.3 copy.30
  (1 shorter events, 0.0 us)
Async XLA Ops:
  3.9 139.2 %copy-start.1 = (f32[1280]{0:T(1024)S(1)}, f32[1280]{0:T(1024)}, u32[]{:S(2)}) copy-start(f32[1280]{0:T(1024)} %param.17) | copy-start | bytes 15364
  3.9 139.2 %copy-start.3 = (f32[1280]{0:T(1024)S(1)}, f32[1280]{0:T(1024)}, u32[]{:S(2)}) copy-start(f32[1280]{0:T(1024)} %param.19) | copy-start | bytes 15364
  3.9 139.2 %copy-start.4 = (f32[1280]{0:T(1024)S(1)}, f32[1280]{0:T(1024)}, u32[]{:S(2)}) copy-start(f32[1280]{0:T(1024)} %param.18) | copy-start | bytes 15364
  3.9 140.6 %copy-start.2 = (f32[1408]{0:T(1024)S(1)}, f32[1408]{0:T(1024)}, u32[]{:S(2)}) copy-start(f32[1408]{0:T(1024)} %param.20) | copy-start | bytes 16900
  3.9 140.6 %copy-start.5 = (f32[1408]{0:T(1024)S(1)}, f32[1408]{0:T(1024)}, u32[]{:S(2)}) copy-start(f32[1408]{0:T(1024)} %param.22) | copy-start | bytes 16900
  3.9 140.6 %copy-start.6 = (f32[1408]{0:T(1024)S(1)}, f32[1408]{0:T(1024)}, u32[]{:S(2)}) copy-start(f32[1408]{0:T(1024)} %param.21) | copy-start | bytes 16900
  145.9 3.3 %copy-start = (f32[8,2,256,128]{3,2,1,0:T(8,128)S(1)}, f32[8,2,256,128]{3,2,1,0:T(8,128)}, u32[]{:S(2)}) copy-start(f32[8,2,256,128]{3,2,1,0:T(8,128)} %get-tuple-element.42) | copy-start | bytes 6291460

commit v2 on v1

--- a/solution.py
+++ b/solution.py
@@ -65,8 +65,9 @@
     x_hbm,
     frc_hbm,
     cot_hbm,
-    wsh_hbm,
-    small_hbm,
+    mat_hbm,
+    bias_hbm,
+    lat_hbm,
     lc_hbm,
     bk_hbm,
     bi_hbm,
@@ -79,8 +80,10 @@
     cv,
     ov,
     gv,
+    mat,
     wsh,
-    small,
+    bias,
+    lat_in,
     lc,
     bk,
     bi,
@@ -96,13 +99,16 @@
     lp,
     lqt,
     lpt,
+    rows,
     cx,
     pex,
     fac,
     fil,
     kap,
     qs,
-    wg,
+    wz,
+    wrow,
+    wb,
     wflat,
     we,
     ww,
@@ -118,18 +124,23 @@
     dwd,
     db,
     gf,
+    rk,
+    rh,
     rx,
     s1r,
-    rp,
+    ry,
     s2r,
-    rq,
+    rw,
     blk,
+    wide,
     pps,
     ppr,
     px,
     pxr,
     pz,
     pzr,
+    pzl,
+    pzlr,
     tot,
     pgr,
     fin,
@@ -145,6 +156,7 @@
     me = lax.axis_index("lat")
     zme = lax.div(me, 8)
     bme = lax.rem(me, 8)
+    yme = lax.div(bme, 2)
     odd = lax.rem(me, 2)
 
     def x_copy(ch):
@@ -153,12 +165,13 @@
 
     loads = [
         pltpu.make_async_copy(bk_hbm, bk, isem.at[0]),
-        pltpu.make_async_copy(wsh_hbm, wsh, isem.at[1]),
-        pltpu.make_async_copy(small_hbm, small, isem.at[2]),
+        pltpu.make_async_copy(mat_hbm, mat, isem.at[1]),
+        pltpu.make_async_copy(bias_hbm, bias, isem.at[2]),
         pltpu.make_async_copy(lc_hbm, lc, isem.at[3]),
         pltpu.make_async_copy(bi_hbm, bi, isem.at[4]),
         pltpu.make_async_copy(frc_hbm, fv, isem.at[5]),
         pltpu.make_async_copy(cot_hbm, cv, isem.at[6]),
+        pltpu.make_async_copy(lat_hbm, lat_in, isem.at[9]),
     ]
     loads[0].start()
     for ch in range(CH):
@@ -268,128 +281,117 @@
             sides = jnp.concatenate([xv[2 * ch, row], xv[2 * ch + 1, row]], axis=1)
             found.append(dot(bk[row], sides.astype(bf16)))
         s1[ch] = pack(found[0], found[1])
-
-        @pl.when(ch == 0)
-        def _():
-            loads[1].wait()
-            wg[xme, zme, bme] = wsh[...]
-            pl.semaphore_wait(barrier, LATS - 1 + XS - 1)
-            to_column(wsh, wg.at[xme, zme, bme], 0)
-
-        @pl.when(ch == 1)
-        def _():
-            drain(wg.at[0, pl.ds(0, 7), 0], gr.at[0])
-            to_plane(lambda other: wg.at[xme, :, bme], wg.at[xme, :, bme], 1)
-
-        @pl.when(ch == 2)
-        def _():
-            drain(wg.at[0, :, pl.ds(0, 7)], gr.at[1])
-            to_line(lambda other: wg.at[xme], wg.at[xme], 2)
-
-        exchange(0, s1, r1, ch)
         return carry
 
     lax.fori_loop(0, CH, analyse, 0)
 
-    for load in loads[2:5]:
-        load.wait()
-    lane_col = lax.broadcasted_iota(jnp.int32, (128, 1024), 1)
-    lat_index = lax.broadcasted_iota(jnp.int32, (128, 1024), 0)
-    row_bit = lax.rem(lax.rem(lax.div(lane_col, 4), 2) + odd, 2)
-    one_hot = jnp.where(lat_index == 2 * lax.div(lane_col, 16) + row_bit, 1.0, 0.0).astype(bf16)
-    lat = dot(small[16:24, :].astype(bf16), one_hot)[0:1, :]
+    for number in (1, 2, 3, 7):
+        loads[number].wait()
+    sub = lax.broadcasted_iota(jnp.int32, (128, 128), 0)
+    lane = lax.broadcasted_iota(jnp.int32, (128, 128), 1)
+    row_of_lane = 2 * lax.rem(lane, LATS) + lax.rem(lax.div(lane, LATS) + odd, 2)
+    one_hot = jnp.where(sub == row_of_lane, 1.0, 0.0).astype(bf16)
+    lat_rows = jnp.broadcast_to(lat_in[...].astype(f32), (8, 128)).astype(bf16)
+    lat = dot(lat_rows, one_hot)[0:1, :]
     phi = (lat + 0.5) * (math.pi / NLAT) - 0.5 * math.pi
     mu = jnp.sin(phi)
     cos_phi = jnp.cos(phi)
-
-    sub = lax.broadcasted_iota(jnp.int32, (128, 128), 0)
-    lane = lax.broadcasted_iota(jnp.int32, (128, 128), 1)
+    log_cos = jnp.log(cos_phi)
     m_zero = 2 * me
     k_safe = jnp.maximum(sub, 1).astype(f32)
     logs = jnp.log((2.0 * k_safe + 1.0) / (2.0 * k_safe))
-    starts = []
+    firsts = []
     for slot in range(2):
+        wave = (m_zero + slot).astype(f32)
         below = (sub >= 1) & (sub <= m_zero + slot)
-        starts.append(
-            -0.5 * math.log(2.0) + 0.5 * jnp.sum(jnp.where(below, logs, 0.0), axis=0, keepdims=True)
+        total = jnp.sum(jnp.where(below, logs, 0.0), axis=0, keepdims=True)
+        firsts.append(jnp.exp(-0.5 * math.log(2.0) + 0.5 * total + wave * log_cos))
+        pex[slot, 0:1, :] = firsts[slot]
+        degree = wave + sub.astype(f32)
+        less = degree - 1.0
+        square = wave * wave
+        gap = jnp.where(sub == 0, 1.0, degree * degree - square)
+        fac[slot, 0] = jnp.sqrt(jnp.maximum((4.0 * degree * degree - 1.0) / gap, 0.0))
+        fac[slot, 1] = jnp.sqrt(
+            jnp.maximum((less * less - square) / (4.0 * less * less - 1.0), 0.0)
         )
-    slot_lane = lax.rem(lax.div(lane, 2), 2)
-    start = jnp.where(slot_lane[0:1] == 0, starts[0], starts[1])
-    start = jnp.concatenate([start] * 8, axis=1)
-    m_lane = (m_zero + slot_lane).astype(f32)
-    m_wide = jnp.concatenate([m_lane[0:1]] * 8, axis=1)
-    first = jnp.exp(start + m_wide * jnp.log(cos_phi))
-    degree = m_lane + sub.astype(f32)
-    less = degree - 1.0
-    m_square = m_lane * m_lane
-    gap = jnp.where(sub == 0, 1.0, degree * degree - m_square)
-    fac[0] = jnp.sqrt(jnp.maximum((4.0 * degree * degree - 1.0) / gap, 0.0))
-    fac[1] = jnp.sqrt(jnp.maximum((less * less - m_square) / (4.0 * less * less - 1.0), 0.0))
-    pex[0:1, :] = first
-
-    def advance(n, pair):
-        latest, earlier = pair
-        up = jnp.concatenate([fac[0, pl.ds(n, 1), :]] * 8, axis=1)
-        down = jnp.concatenate([fac[1, pl.ds(n, 1), :]] * 8, axis=1)
-        now = up * (mu * latest - down * earlier)
-        pex[pl.ds(n, 1), :] = now
-        return (now, latest)
-
-    lax.fori_loop(1, MW, advance, (first, jnp.zeros_like(first)))
-
-    for slot in range(2):
-        deg = (m_zero + slot + sub).astype(f32)
-        live = deg < MW - 0.5
-        ratio = deg / MW
+        live = degree < MW - 0.5
+        ratio = degree / MW
         ratio = ratio * ratio
         ratio = ratio * ratio
         fil[slot] = jnp.where(live, jnp.exp(-(ratio * ratio)), 0.0)
-        kap[slot] = deg * (deg + 1.0) / (MW * (MW - 1.0))
-
-    n_wide = lax.broadcasted_iota(jnp.int32, (128, 1024), 0)
-    keep = n_wide.astype(f32) + m_wide < MW - 0.5
-    weight = jnp.where(m_wide == 0.0, 1.0, 2.0)
-    poly = jnp.where(keep, pex[...], 0.0)
-    synth = poly * weight
-    quad = poly * ((math.pi / NLAT) * cos_phi)
-    anal = quad * (1.0 / NLON)
-    synth_t = synth.T
-    anal_t = anal.T
-    lane16 = lax.rem(lane_col[0:1], 16)
-    row16 = lax.rem(lax.broadcasted_iota(jnp.int32, (1024, 128), 0), 16)
-
-    def chosen(sixteen, combo):
-        return (
-            (lax.div(sixteen, 8) == combo // 4)
-            & (lax.rem(lax.div(sixteen, 2), 2) == (combo // 2) % 2)
-            & (lax.rem(sixteen, 2) == combo % 2)
-        )
-
-    for combo in range(8):
-        part = slice(combo * 128, combo * 128 + 128)
-        mine = chosen(lane16, combo)
-        lp[part, :] = jnp.where(mine, synth, 0.0).astype(bf16)
-        lq[part, :] = jnp.where(mine, anal, 0.0).astype(bf16)
-        mine_t = chosen(row16, combo)
-        lpt[:, part] = jnp.where(mine_t, synth_t, 0.0).astype(bf16)
-        lqt[:, part] = jnp.where(mine_t, anal_t, 0.0).astype(bf16)
-    zero_wave = jnp.sum(jnp.where(chosen(lane16, 0), quad, 0.0), axis=1, keepdims=True)
-    zero_wave = jnp.where(me == 0, zero_wave, 0.0)
-    qs[...] = jnp.broadcast_to(zero_wave, (128, 128))
+        kap[slot] = degree * (degree + 1.0) / (MW * (MW - 1.0))
+
+    def advance(n, pairs):
+        following = []
+        for slot in range(2):
+            latest, earlier = pairs[slot]
+            up = fac[slot, 0, pl.ds(n, 1), :]
+            down = fac[slot, 1, pl.ds(n, 1), :]
+            now = up * (mu * latest - down * earlier)
+            pex[slot, pl.ds(n, 1), :] = now
+            following.append((now, latest))
+        return tuple(following)
+
+    lax.fori_loop(
+        1, MW, advance, tuple((firsts[slot], jnp.zeros((1, 128), f32)) for slot in range(2))
+    )
+
+    for slot in range(2):
+        keep = m_zero + slot + sub < MW
+        poly = jnp.where(keep, pex[slot], 0.0)
+        synth = poly * jnp.where(m_zero + slot == 0, 1.0, 2.0)
+        quad = poly * ((math.pi / NLAT) * cos_phi)
+        anal = quad * (1.0 / NLON)
+        lp[slot] = synth.astype(bf16)
+        lq[slot] = anal.astype(bf16)
+        lpt[slot] = synth.T.astype(bf16)
+        lqt[slot] = anal.T.astype(bf16)
+        if slot == 0:
+            zero_wave = jnp.sum(quad, axis=1, keepdims=True)
+            zero_wave = jnp.where(me == 0, zero_wave, 0.0)
+            qs[...] = jnp.broadcast_to(zero_wave, (128, 128))
     lc_top, lc_low = halves(lc[...])
     lch[0] = lc_top
     lch[1] = lc_low
 
-    drain(wg.at[pl.ds(0, 3)], gr.at[2])
-
-    def spread(group, carry):
-        tiles = wg[lax.div(group, 8), lax.rem(group, 8)].astype(f32)
-        rows = wflat.at[pl.ds(pl.multiple_of(group * 80, 8), 80)]
+    wsh[...] = jnp.concatenate([mat[...], jnp.zeros((6, 128), f32)], axis=0).astype(bf16)
+    wz[zme] = wsh[...]
+    pl.semaphore_wait(barrier, LATS - 1 + XS - 1)
+    to_column(wsh, wz.at[zme], 0)
+    exchange(0, s1, r1, 0)
+    exchange(0, s1, r1, 1)
+
+    drain(wz.at[pl.ds(0, 7)], gr.at[0])
+    tiles = wz[...].astype(f32)
+    for z in range(8):
+        wrow[z * 10 : z * 10 + 10, :] = tiles[z, 0:10, :]
+    wb[xme, bme] = wrow[...].astype(bf16)
+    to_plane(lambda other: wb.at[xme, bme], wb.at[xme, bme], 1)
+    exchange(0, s1, r1, 2)
+
+    drain(wb.at[0, pl.ds(0, 7)], gr.at[1])
+    own_part = wb.at[xme, pl.ds(4 * odd, 4)]
+    to_line(lambda other: own_part, own_part, 2)
+    exchange(0, s1, r1, 3)
+
+    drain(wb.at[pl.ds(0, 3), pl.ds(0, 4)], gr.at[2])
+    for step in range(1, XS):
+        part = wb.at[lax.rem(xme + step, XS), pl.ds(4 * odd, 4)]
+        lat_copy(part, part, gs.at[11], gr.at[11], me + 1 - 2 * odd).start()
+
+    drain(wb.at[pl.ds(0, 3), pl.ds(0, 4)], gr.at[11])
+
+    def spread(line, carry):
         for b in range(8):
-            rows[b * 10 : b * 10 + 10, :] = tiles[b, 0:10, :]
+            tile = wb[line, b].astype(f32)
+            for z in range(8):
+                target = wflat.at[pl.ds(pl.multiple_of(line * 640, 8), 640)]
+                begin = z * 80 + b * 10
+                target[begin : begin + 10, :] = tile[z * 10 : z * 10 + 10, :]
         return carry
 
-    lax.fori_loop(0, 32, spread, 0)
+    lax.fori_loop(0, XS, spread, 0)
     we[...] = wflat[0:128, :].astype(bf16)
     for layer in range(4):
         for side in range(2):
@@ -399,6 +401,7 @@
             ].astype(bf16)
     w5[...] = wflat[2176:2432, :].astype(bf16)
     wd[...] = wflat[2432:2560, :].astype(bf16)
+    loads[4].wait()
     dwe[...] = jnp.zeros_like(dwe)
     dww[...] = jnp.zeros_like(dww)
     dw5[...] = jnp.zeros_like(dw5)
@@ -411,26 +414,59 @@
         return product(top, lch[0]) + product(top, lch[1]) + product(low, lch[0])
 
     def per_slot(table):
-        both = jnp.concatenate([table[0], table[0], table[1], table[1]], axis=0)
-        return jnp.concatenate([both, both], axis=0)
-
-    zero_combos = (0, 4)
-
-    def add_zero_wave(value, extra):
-        blocks = [value[c * 128 : c * 128 + 128] for c in range(8)]
-        for c in zero_combos:
-            blocks[c] = blocks[c] + extra
-        return jnp.concatenate(blocks, axis=0)
+        return jnp.concatenate([table[0]] * 4 + [table[1]] * 4, axis=0)
+
+    def gather_rows(tiles, slot):
+        if slot == 0:
+            rows[...] = tiles.astype(f32).reshape(1024, 128)
+        sides = []
+        for globe in range(2):
+            for part in range(2):
+                begin = globe * 8 + slot * 2 + part
+                sides.append(
+                    jnp.concatenate(
+                        [rows[pl.ds(begin + 4 * k, LATS, stride=16), :] for k in range(2)], axis=0
+                    )
+                )
+        return jnp.concatenate(sides, axis=1).astype(bf16)
+
+    def to_coefficients(table, tiles):
+        blocks = []
+        for slot in range(2):
+            found = dot(table[slot], gather_rows(tiles, slot))
+            blocks += [found[:, k * 128 : k * 128 + 128] for k in range(4)]
+        return blocks
+
+    def to_tiles(table, blocks):
+        for slot in range(2):
+            wide_low = jnp.concatenate(blocks[4 * slot : 4 * slot + 4], axis=1).astype(bf16)
+            found = dot(table[slot], wide_low)
+            for globe in range(2):
+                for part in range(2):
+                    begin = globe * 8 + slot * 2 + part
+                    lanes = slice((globe * 2 + part) * 128, (globe * 2 + part) * 128 + 128)
+                    for k in range(2):
+                        rows[pl.ds(begin + 4 * k, LATS, stride=16), :] = found[
+                            k * LATS : k * LATS + LATS, lanes
+                        ]
+        return rows[...].astype(bf16).reshape(LATS, 16, 128)
+
+    def cut(value):
+        return [value[c * 128 : c * 128 + 128] for c in range(8)]
 
     def dynamics(ch, carry):
         arrived(0, r1, ch)
-        coef = dot(lq[...], r1[ch].reshape(1024, 128))
+        blocks = to_coefficients(lq, r1[ch])
+        coef = jnp.concatenate(blocks, axis=0)
         coef_low = coef.astype(bf16)
         cx[ch] = coef_low
-        coef = coef + dot(coef_low, we[...])
-        coef = add_zero_wave(coef, qs[...] * small[0:1, :])
+        blocks = cut(coef + dot(coef_low, we[...]))
+        constant = qs[...] * bias[0:1, :]
+        blocks[0] = blocks[0] + constant
+        blocks[2] = blocks[2] + constant
+        coef = jnp.concatenate(blocks, axis=0)
         coef = per_slot(fil) * (coef - per_slot(kap) * couple(coef, False))
-        s2[ch] = dot(lpt[...], coef.astype(bf16)).astype(bf16).reshape(LATS, 16, 128)
+        s2[ch] = to_tiles(lpt, cut(coef))
         exchange(1, s2, r2, ch)
         return carry
 
@@ -450,7 +486,7 @@
     c_one = 0.044715
 
     def bias_row(index, count):
-        return jnp.concatenate([small[index + k : index + k + 1, :] for k in range(count)], axis=1)
+        return jnp.concatenate([bias[index + k : index + k + 1, :] for k in range(count)], axis=1)
 
     def add_bias(index, value):
         total = jnp.sum(value, axis=0, keepdims=True)
@@ -511,17 +547,17 @@
 
     def adjoint(ch):
         arrived(2, r3, ch)
-        back = per_slot(fil) * dot(lp[...], r3[ch].reshape(1024, 128))
+        back = jnp.concatenate(to_coefficients(lp, r3[ch]), axis=0)
+        back = per_slot(fil) * back
         back = back - couple(per_slot(kap) * back, True)
         back_low = back.astype(bf16)
         dwe[...] += dot_tn(cx[ch], back_low)
-        flat = qs[...] * (back[0:128] + back[512:640])
+        flat = qs[...] * (back[0:128] + back[256:384])
         db[0:1, :] += jnp.sum(flat, axis=0, keepdims=True)
         back = back + dot_nt(back_low, we[...])
-        s4[ch] = dot(lqt[...], back.astype(bf16)).astype(bf16).reshape(LATS, 16, 128)
-        exchange(3, s4, r4, ch)
-
-    def grad_line():
+        s4[ch] = to_tiles(lqt, cut(back))
+
+    def grad_core():
         gf[0:128, :] = jnp.zeros((128, 128), f32)
         for layer in range(4):
             for side in range(2):
@@ -529,89 +565,124 @@
                 gf[pl.ds(begin, 256, stride=2), :] = dww[layer, :, side * 128 : side * 128 + 128]
         gf[2176:2432, :] = dw5[...]
         gf[2432:2560, :] = dwd[...]
-        to_line(lambda other: gf.at[pl.ds(pl.multiple_of(other * 640, 8), 640)], rx.at[xme], 3)
-
-    def grad_plane():
+
+        def one(part, carry):
+            begin = pl.multiple_of(part * 160 + 80 * (1 - odd), 8)
+            lat_copy(
+                gf.at[pl.ds(begin, 80)], rk.at[part], gs.at[12], gr.at[12], me + 1 - 2 * odd
+            ).start()
+            return carry
+
+        lax.fori_loop(0, 16, one, 0)
+
+    def grad_line():
+        drain(rk, gr.at[12])
+
+        def one(part, carry):
+            begin = pl.multiple_of(part * 160 + 80 * odd, 8)
+            total = rk[part] + gf[pl.ds(begin, 80), :]
+            rk[part] = total
+            rh[part] = total.astype(bf16)
+            return carry
+
+        lax.fori_loop(0, 16, one, 0)
+        to_line(lambda other: rh.at[pl.ds(4 * other, 4)], rx.at[xme], 3)
+
+    def grad_row():
         drain(rx.at[pl.ds(0, 3)], gr.at[3])
-        total = gf[pl.ds(pl.multiple_of(xme * 640, 8), 640), :]
+        total = rk[pl.ds(4 * xme, 4)]
         for step in range(1, XS):
-            total = total + rx[lax.rem(xme + step, XS)]
+            total = total + rx[lax.rem(xme + step, XS)].astype(f32)
         s1r[...] = total
-        to_plane(lambda other: s1r.at[pl.ds(pl.multiple_of(other * 80, 8), 80)], rp.at[bme], 4)
-
-    def grad_turn():
-        drain(rp.at[pl.ds(0, 7)], gr.at[4])
-        total = s1r[pl.ds(pl.multiple_of(bme * 80, 8), 80), :]
-        for step in range(1, 8):
-            total = total + rp[lax.rem(bme + step, 8)]
-        s2r[...] = total
-
+        for step in range(1, 4):
+            other = lax.rem(yme + step, 4)
+            peer = zme * 8 + other * 2 + odd
+            lat_copy(s1r.at[other], ry.at[yme], gs.at[4], gr.at[4], peer).start()
+
+    def grad_column():
+        drain(ry.at[pl.ds(0, 3)], gr.at[4])
+        total = s1r[yme]
+        for step in range(1, 4):
+            total = total + ry[lax.rem(yme + step, 4)]
+        for b in range(8):
+            begin = 8 * (10 * b // 8)
+            s2r[b] = total[begin : begin + 16].astype(bf16)
+        for step in range(8):
+            other = lax.rem(bme + step, 8)
+            peer = bme * 8 + other
+
+            @pl.when(peer != me)
+            def _():
+                lat_copy(
+                    s2r.at[other], rw.at[zme], gs.at[5], gr.at[5], peer
+                ).start()
+
+            @pl.when(peer == me)
+            def _():
+                rw[zme] = s2r[other]
+
+    def turn_bytes(sem):
         @pl.when(bme == zme)
         def _():
-            rq[bme] = s2r[...]
+            drain(rw.at[pl.ds(0, 7)], sem)
 
         @pl.when(bme != zme)
         def _():
-            lat_copy(s2r, rq.at[zme], gs.at[5], gr.at[5], bme * 8 + zme).start()
-
-    def grad_share():
-        @pl.when(bme != zme)
+            drain(rw, sem)
+
+    def grad_block():
+        turn_bytes(gr.at[5])
+        total = rw[0].astype(f32)
+        for z in range(1, 8):
+            total = total + rw[z].astype(f32)
+        row = lax.broadcasted_iota(jnp.int32, (16, 128), 0)
+        begin = 2 * lax.rem(bme, 4)
+        total = jnp.where((row >= begin) & (row < begin + 10), total, 0.0)
+        blk[...] = total
+        return total * total
+
+    def forward_steps(ch, carry):
+        arrived(1, r2, ch)
+        columns(ch)
+        return carry
+
+    lax.fori_loop(0, CH, forward_steps, 0)
+    grad_core()
+
+    def adjoint_steps(ch, carry):
+        adjoint(ch)
+
+        @pl.when(ch == 0)
         def _():
-            drain(s2r, gr.at[5])
-
-        to_plane(lambda other: rq.at[bme], rq.at[bme], 6)
-
-    def grad_block():
-        drain(rq.at[pl.ds(0, 7)], gr.at[6])
-        total = rq[0]
-        for b in range(1, 8):
-            total = total + rq[b]
-        blk[...] = total
-
-    def middle_steps(t, carry):
-        @pl.when(t < CH)
+            exchange(3, s4, r4, 0)
+            grad_line()
+
+        @pl.when(ch == 1)
         def _():
-            arrived(1, r2, t)
-            columns(t)
-
-        @pl.when(t == CH - 1)
+            grad_row()
+
+        @pl.when(ch == 2)
         def _():
-            grad_line()
-
-        @pl.when(t >= 2)
-        def _():
-            adjoint(t - 2)
-
-        @pl.when(t == CH)
-        def _():
-            grad_plane()
-
-        @pl.when(t == CH + 1)
-        def _():
-            grad_turn()
+            grad_column()
 
         return carry
 
-    lax.fori_loop(0, CH + 2, middle_steps, 0)
-
-    grad_share()
+    lax.fori_loop(0, CH, adjoint_steps, 0)
+
     for b in range(8):
         pps[b, 0:16, :] = dwe[b * 16 : b * 16 + 16, :]
         pps[b, 16:32, :] = db[...]
     to_plane(lambda other: pps.at[other], ppr.at[bme], 7)
+    exchange(3, s4, r4, 1)
 
     def last_line():
-        grad_block()
         drain(ppr.at[pl.ds(0, 7)], gr.at[7])
         total = pps[bme]
         for step in range(1, 8):
             total = total + ppr[lax.rem(bme + step, 8)]
         px[0:32, :] = total
-        square = blk[0:8, :] * blk[0:8, :]
-        for k in range(1, 10):
-            piece = blk[8 * k : 8 * k + 8, :]
-            square = square + piece * piece
-        px[32:40, :] = square
+        square = grad_block()
+        px[32:40, :] = square[0:8] + square[8:16]
         to_line(lambda other: px, pxr.at[xme], 8)
 
     def last_column():
@@ -619,53 +690,81 @@
         total = px[...]
         for step in range(1, XS):
             total = total + pxr[lax.rem(xme + step, XS)]
-        pz[...] = total
+        pzl[...] = total[0:16].astype(bf16)
+        pz[...] = jnp.zeros((8, 128), f32)
+        two_rows = jnp.zeros((2, 128), f32)
+        for k in range(8):
+            chosen = jnp.where(bme == k, 1.0, 0.0)
+            two_rows = two_rows + chosen * total[16 + 2 * k : 18 + 2 * k]
+        pz[0:2, :] = two_rows
+        pz[2:3, :] = jnp.sum(total[32:40], axis=0, keepdims=True)
         to_column(pz, pzr.at[zme], 9)
+        to_column(pzl, pzlr.at[zme], 13)
 
     def last_plane():
         drain(pzr.at[pl.ds(0, 7)], gr.at[9])
+        drain(pzlr.at[pl.ds(0, 7)], gr.at[13])
         total = pz[...]
+        wide_total = pzl[...].astype(f32)
         for step in range(1, 8):
             total = total + pzr[lax.rem(zme + step, 8)]
-        tot[...] = total
-        pgr[bme] = tot[0:16, :]
-        to_plane(lambda other: tot.at[pl.ds(0, 16)], pgr.at[bme], 10)
+            wide_total = wide_total + pzlr[lax.rem(zme + step, 8)].astype(f32)
+        tot[0:16, :] = wide_total
+        tot[16:24, :] = total
+        pgr[bme] = tot[...]
+        to_plane(lambda other: tot, pgr.at[bme], 10)
+
 
     def finish(ch, carry):
-        @pl.when(ch == 1)
-        def _():
-            last_line()
-
-        @pl.when(ch == 2)
-        def _():
-            last_column()
-
-        @pl.when(ch == 3)
-        def _():
-            last_plane()
-
         arrived(3, r4, ch)
         for row in range(2):
             grid = dot(bi[row], unpack(r4[ch], row))
             gv[2 * ch, row] = grid[:, 0:128]
             gv[2 * ch + 1, row] = grid[:, 128:256]
         out_copy[1](ch).start()
+
+        @pl.when(ch == 0)
+        def _():
+            exchange(3, s4, r4, 2)
+            last_line()
+            last_column()
+
+        @pl.when(ch == 1)
+        def _():
+            exchange(3, s4, r4, 3)
+
+        @pl.when(ch == 2)
+        def _():
+            last_plane()
+
         return carry
 
     lax.fori_loop(0, CH, finish, 0)
 
     drain(pgr.at[pl.ds(0, 7)], gr.at[10])
-    enc = pgr[...].reshape(128, 128)
-    at_zero = jnp.where((xme == 0) & (zme == 0), 1.0, 0.0)
-    at_one = jnp.where((xme == 0) & (zme == 1), 1.0, 0.0)
-    blk[...] += at_zero * enc[0:80]
-    blk[0:48, :] += at_one * enc[80:128]
-    bias_total = tot[16:32, :]
+    enc = pgr[:, 0:16, :].reshape(128, 128)
+    row = lax.broadcasted_iota(jnp.int32, (128, 128), 0)
+    first_row = 640 * xme + 10 * me
+    wide[0:128, :] = jnp.where((row >= first_row) & (row < first_row + 10), enc, 0.0)
+    wide[128:160, :] = jnp.zeros((32, 128), f32)
+
+    @pl.when((xme == 0) & (zme < 2))
+    def _():
+        begin = pl.multiple_of(80 * zme + 8 * lax.div(10 * bme, 8), 8)
+        blk[...] += wide[pl.ds(begin, 16), :]
+
+    for b in range(8):
+        fin[2 * b : 2 * b + 2, :] = pgr[b, 16:18, :]
+    bias_total = fin[0:16, :]
     squares = (
-        jnp.sum(tot[32:40, :]) + jnp.sum(enc * enc) + jnp.sum(bias_total * bias_total)
+        jnp.sum(pgr[:, 18, :]) + jnp.sum(enc * enc) + jnp.sum(bias_total * bias_total)
     )
-    fin[0:16, :] = bias_total
-    fin[16:24, :] = jnp.zeros((8, 128), f32) + squares
+    norm = jnp.sqrt(jnp.zeros((8, 128), f32) + squares)
+    clip = jnp.minimum(1.0, clip_norm / (norm + 1e-06))
+    both_clip = jnp.concatenate([clip, clip], axis=0)
+    fin[0:16, :] = bias_total * both_clip
+    fin[16:24, :] = norm
+    blk[...] = blk[...] * both_clip
     last = [
         pltpu.make_async_copy(blk, blk_hbm, isem.at[7]),
         pltpu.make_async_copy(fin, fin_hbm, isem.at[8]),
@@ -676,20 +775,19 @@
     for phase, src in enumerate((s1, s2, s3, s4)):
         for ch in range(CH):
             drain(src.at[ch, pl.ds(0, LATS - 1)], ssem.at[phase, ch])
-    drain(wg.at[0, pl.ds(0, 7), 0], gs.at[0])
-    drain(wg.at[0, :, pl.ds(0, 7)], gs.at[1])
-    drain(wg.at[pl.ds(0, 3)], gs.at[2])
+    drain(wz.at[pl.ds(0, 7)], gs.at[0])
+    drain(wb.at[0, pl.ds(0, 7)], gs.at[1])
+    drain(wb.at[pl.ds(0, 3), pl.ds(0, 4)], gs.at[2])
+    drain(wb.at[pl.ds(0, 3), pl.ds(0, 4)], gs.at[11])
+    drain(rk, gs.at[12])
     drain(rx.at[pl.ds(0, 3)], gs.at[3])
-    drain(rp.at[pl.ds(0, 7)], gs.at[4])
-
-    @pl.when(bme != zme)
-    def _():
-        drain(s2r, gs.at[5])
-
-    drain(rq.at[pl.ds(0, 7)], gs.at[6])
+    drain(ry.at[pl.ds(0, 3)], gs.at[4])
+
+    turn_bytes(gs.at[5])
     drain(ppr.at[pl.ds(0, 7)], gs.at[7])
     drain(pxr.at[pl.ds(0, 3)], gs.at[8])
     drain(pzr.at[pl.ds(0, 7)], gs.at[9])
+    drain(pzlr.at[pl.ds(0, 7)], gs.at[13])
     drain(pgr.at[pl.ds(0, 7)], gs.at[10])
     for ch in range(CH):
         out_copy[0](ch).wait()
@@ -723,14 +821,6 @@
     lat_of_row,
     step_count,
 ):
-    wsh = jnp.pad(mat_master.reshape(10, 128), ((0, 6), (0, 0))).astype(bf16)
-    small = jnp.concatenate(
-        [
-            jnp.pad(bias_master.reshape(BIAS_ROWS, 128), ((0, 5), (0, 0))),
-            jnp.broadcast_to(lat_of_row.astype(f32)[None, :], (8, 128)),
-        ],
-        axis=0,
-    )
     both, turned = zonal_tables()
     any_spec = pl.BlockSpec(memory_space=pl.ANY)
     big = (8, 2, NLON, C)
@@ -742,20 +832,25 @@
         vm(big, f32),
         vm(big, f32),
         vm(big, f32),
+        vm((10, 128), f32),
         vm((16, 128), bf16),
-        vm((24, 128), f32),
+        vm((BIAS_ROWS, 128), f32),
+        vm((1, 128), jnp.int32),
         vm((128, 128), f32),
         vm((2, 256, 256), bf16),
         vm((2, 256, 256), bf16),
         *[vm(tiles, bf16) for _ in range(8)],
-        *[vm((1024, 1024), bf16) for _ in range(4)],
+        *[vm((2, 128, 128), bf16) for _ in range(4)],
+        vm((1024, 128), f32),
         vm((CH, 1024, 128), bf16),
-        vm((128, 1024), f32),
         vm((2, 128, 128), f32),
+        vm((2, 2, 128, 128), f32),
         vm((2, 128, 128), f32),
         vm((2, 128, 128), f32),
         vm((128, 128), f32),
-        vm((XS, 8, 8, 16, 128), bf16),
+        vm((8, 16, 128), bf16),
+        vm((80, 128), f32),
+        vm((XS, 8, 80, 128), bf16),
         vm((2560, 128), f32),
         vm((128, 128), bf16),
         vm((4, 256, 256), bf16),
@@ -771,38 +866,43 @@
         vm((128, 128), f32),
         vm((16, 128), f32),
         vm((2560, 128), f32),
-        vm((XS, 640, 128), f32),
-        vm((640, 128), f32),
-        vm((8, 80, 128), f32),
-        vm((80, 128), f32),
-        vm((8, 80, 128), f32),
-        vm((80, 128), f32),
+        vm((16, 80, 128), f32),
+        vm((16, 80, 128), bf16),
+        vm((XS, 4, 80, 128), bf16),
+        vm((4, 80, 128), f32),
+        vm((4, 80, 128), f32),
+        vm((8, 16, 128), bf16),
+        vm((8, 16, 128), bf16),
+        vm((16, 128), f32),
+        vm((160, 128), f32),
         vm((8, 32, 128), f32),
         vm((8, 32, 128), f32),
         vm((40, 128), f32),
         vm((XS, 40, 128), f32),
-        vm((40, 128), f32),
-        vm((8, 40, 128), f32),
-        vm((40, 128), f32),
-        vm((8, 16, 128), f32),
+        vm((8, 128), f32),
+        vm((8, 8, 128), f32),
+        vm((16, 128), bf16),
+        vm((8, 16, 128), bf16),
+        vm((24, 128), f32),
+        vm((8, 24, 128), f32),
         vm((24, 128), f32),
         pltpu.SemaphoreType.DMA((CH,)),
-        pltpu.SemaphoreType.DMA((9,)),
+        pltpu.SemaphoreType.DMA((10,)),
         pltpu.SemaphoreType.DMA((2, CH)),
         pltpu.SemaphoreType.DMA((4, CH)),
         pltpu.SemaphoreType.DMA((4, CH)),
-        pltpu.SemaphoreType.DMA((11,)),
-        pltpu.SemaphoreType.DMA((11,)),
+        pltpu.SemaphoreType.DMA((14,)),
+        pltpu.SemaphoreType.DMA((14,)),
     ]
     state_out, state_grad, block, final = pl.pallas_call(
         kernel,
         out_shape=(
             jax.ShapeDtypeStruct(big, f32),
             jax.ShapeDtypeStruct(big, f32),
-            jax.ShapeDtypeStruct((80, 128), f32),
+            jax.ShapeDtypeStruct((16, 128), f32),
             jax.ShapeDtypeStruct((24, 128), f32),
         ),
-        in_specs=[any_spec] * 8,
+        in_specs=[any_spec] * 9,
         out_specs=(any_spec,) * 4,
         scratch_shapes=scratch,
         compiler_params=pltpu.CompilerParams(
@@ -816,20 +916,17 @@
         state,
         forcing,
         state_cot,
-        wsh,
-        small,
+        mat_master.reshape(10, 128),
+        bias_master.reshape(BIAS_ROWS, 128),
+        lat_of_row.reshape(1, 128),
         level_coupling,
         jnp.asarray(both),
         jnp.asarray(turned),
     )
 
-    bias_sum = final[0:BIAS_ROWS].reshape(-1)
-    grad_norm = jnp.sqrt(final[16, 0])
-    clip_factor = jnp.minimum(1.0, clip_norm / (grad_norm + 1e-06))
-    place = lax.rem(lax.axis_index("lat"), 8) * 10
-    mat_total = lax.dynamic_slice(block, (place, 0), (10, 128)).reshape(-1)
-    mat_grad = mat_total * clip_factor
-    bias_grad = bias_sum * clip_factor
+    bias_grad = final[0:BIAS_ROWS].reshape(-1)
+    place = 2 * lax.rem(lax.axis_index("lat"), 4)
+    mat_grad = lax.dynamic_slice(block, (place, 0), (10, 128)).reshape(-1)
     steps_done = step_count[0].astype(f32)
     mat_new, mat_moment_new, mat_second_new = adam_update(
         mat_master, mat_moment, mat_second, mat_grad, steps_done
@@ -849,7 +946,7 @@
         bias_new,
         bias_moment_new,
         bias_second_new,
-        grad_norm.reshape(1),
+        final[16, 0:1],
     )
 
 

time: 152 us -> 122 us (0.80)
  Pallas kernels: 137 us -> 112 us
  other arithmetic: 5.34 us -> 2.67 us
  between operations: 3.31 us -> 1.47 us
    pallas_call x1, Pallas kernels: 137 us -> 112 us  [local(): pl.pallas_call(kernel, out_shape=(jax.ShapeDtypeStruct(big, f32), jax.Sha...]
where the time goes in v2:
time: 122 us
  Pallas kernels  112 us (92%)
  local copies, waits for them, and re-layouts  5.79 us (5%)
  other arithmetic  2.67 us (2%)
  between operations  1.47 us (1%)
    pallas_call x1, Pallas kernels, local(): pl.pallas_call(kernel, out_shape=(jax.ShapeDtypeStruct(big, f32), jax.Sha...  112 us
    unnamed x16, local copies, waits for them, and re-layouts  4.61 us

profile of v2, /device:TPU:1, one launch (start us, length us, event | category | flops | bytes accessed | tf_op | source)
XLA Modules:
  0.0 122.1 jit_solution(12873826257609192368)
XLA Ops:
  0.6 0.0 copy-start.1
  0.7 0.0 copy-start.2
  0.7 0.0 copy-start.3
  0.7 0.0 copy-start.4
  0.7 0.0 copy-start.5
  0.7 0.0 copy-start.6
  0.7 112.1 %column_step.1 = (f32[8,2,256,128]{3,2,1,0:T(8,128)}, f32[8,2,256,128]{3,2,1,0:T(8,128)}, f32[16,128]{1,0:T(8,128)}, f32[24,128]{1,0:T(8,128)}) custom-call(f32[8,2,256,128]{3,2,1,0:T(8,128)} %x_hbm.1, bf16[8,2,256,128]{3,2,1,0:T(8,128)(2,1)} %frc_hbm.1, f32[8,2,256,128]{3,2,1,0:T(8,128)} %cot_hbm.1, f32[10,128]{1,0:T(8,128)} %bitcast.12, ...), custom_call_target="tpu_custom_call" | custom-call | flops 16000000000 | bytes 10485760 | tf_op jit(solution)/shard_map/column_step/pallas_call | solution.py:897
  113.6 0.0 copy-done.1
  113.6 0.0 copy-done.2
  113.6 0.0 copy-done.3
  113.6 1.3 %fusion.3 = (bf16[1280]{0:T(1024)(128)(2,1)}, f32[1280]{0:T(1024)}, f32[1280]{0:T(1024)}, f32[1280]{0:T(1024)}, f32[1280]{0:T(1024)}) fusion(f32[1280]{0:T(1024)S(1)} %copy-done.1, f32[]{:T(128)} %bitcast.5, f32[]{:T(128)} %bitcast.4, f32[1280]{0:T(1024)S(1)} %copy-done.2, f32[1280]{0:T(1024)S(1)} %copy-done.3, f32[16,128]{1,0:T(8,128)} %get-tuple-element.18, ...), kind=kLoop, calls=%fused_computation.10 | loop fusion | flops 20480 | bytes 43532 | tf_op jit(solution)/shard_map/convert_element_type | solution.py:942
  115.0 0.0 copy-done.4
  115.0 0.0 copy-done.5
  115.0 0.0 copy-done.6
  115.0 1.3 %multiply_subtract_fusion = (f32[1408]{0:T(1024)}, f32[1408]{0:T(1024)}, f32[1408]{0:T(1024)}, f32[1408]{0:T(1024)}) fusion(f32[1408]{0:T(1024)S(1)} %copy-done.4, f32[]{:T(128)} %bitcast.5, f32[]{:T(128)} %bitcast.4, f32[1408]{0:T(1024)S(1)} %copy-done.5, f32[1408]{0:T(1024)S(1)} %copy-done.6, f32[24,128]{1,0:T(8,128)} %get-tuple-element.19), kind=kLoop, calls=%fused_computation.4 | loop fusion | flops 21120 | bytes 45064 | tf_op jit(solution)/shard_map/sub | solution.py:804
  116.3 1.2 slice.7
  117.5 0.0 copy-start
  117.5 3.3 %copy.29 = f32[8,2,256,128]{3,2,1,0:T(8,128)} copy(f32[8,2,256,128]{3,2,1,0:T(8,128)} %get-tuple-element.41) | data formatting | bytes 4194304
  120.8 0.0 copy-done
  120.8 1.3 %copy.30 = f32[8,2,256,128]{3,2,1,0:T(8,128)} copy(f32[8,2,256,128]{3,2,1,0:T(8,128)S(1)} %copy-done) | data formatting | bytes 4194304
Async XLA Ops:
  0.6 113.0 %copy-start.1 = (f32[1280]{0:T(1024)S(1)}, f32[1280]{0:T(1024)}, u32[]{:S(2)}) copy-start(f32[1280]{0:T(1024)} %param.17) | copy-start | bytes 15364
  0.7 113.0 %copy-start.2 = (f32[1280]{0:T(1024)S(1)}, f32[1280]{0:T(1024)}, u32[]{:S(2)}) copy-start(f32[1280]{0:T(1024)} %param.19) | copy-start | bytes 15364
  0.7 113.0 %copy-start.3 = (f32[1280]{0:T(1024)S(1)}, f32[1280]{0:T(1024)}, u32[]{:S(2)}) copy-start(f32[1280]{0:T(1024)} %param.18) | copy-start | bytes 15364
  0.7 114.3 %copy-start.4 = (f32[1408]{0:T(1024)S(1)}, f32[1408]{0:T(1024)}, u32[]{:S(2)}) copy-start(f32[1408]{0:T(1024)} %param.20) | copy-start | bytes 16900
  0.7 114.3 %copy-start.5 = (f32[1408]{0:T(1024)S(1)}, f32[1408]{0:T(1024)}, u32[]{:S(2)}) copy-start(f32[1408]{0:T(1024)} %param.22) | copy-start | bytes 16900
  0.7 114.3 %copy-start.6 = (f32[1408]{0:T(1024)S(1)}, f32[1408]{0:T(1024)}, u32[]{:S(2)}) copy-start(f32[1408]{0:T(1024)} %param.21) | copy-start | bytes 16900
  117.5 3.3 %copy-start = (f32[8,2,256,128]{3,2,1,0:T(8,128)S(1)}, f32[8,2,256,128]{3,2,1,0:T(8,128)}, u32[]{:S(2)}) copy-start(f32[8,2,256,128]{3,2,1,0:T(8,128)} %get-tuple-element.42) | copy-start | bytes 6291460

commit v3 on v2

--- a/solution.py
+++ b/solution.py
@@ -71,15 +71,13 @@
     lc_hbm,
     bk_hbm,
     bi_hbm,
-    so_hbm,
-    sg_hbm,
-    blk_hbm,
-    fin_hbm,
+    ov,
+    gv,
+    blk,
+    fin,
     xv,
     fv,
     cv,
-    ov,
-    gv,
     mat,
     wsh,
     bias,
@@ -131,7 +129,6 @@
     ry,
     s2r,
     rw,
-    blk,
     wide,
     pps,
     ppr,
@@ -143,10 +140,8 @@
     pzlr,
     tot,
     pgr,
-    fin,
     xsem,
     isem,
-    osem,
     ssem,
     rsem,
     gs,
@@ -221,7 +216,7 @@
 
     def exchange(phase, src, dst, ch):
         def one(step, carry):
-            peer = lax.rem(me + step, LATS)
+            peer = lax.rem(me + 9 * step, LATS)
             lat_copy(
                 src.at[ch, peer], dst.at[ch, me], ssem.at[phase, ch], rsem.at[phase, ch], peer
             ).start()
@@ -274,18 +269,41 @@
 
     loads[0].wait()
 
-    def analyse(ch, carry):
+    def analyse(ch):
         x_copy(ch).wait()
         found = []
         for row in range(2):
             sides = jnp.concatenate([xv[2 * ch, row], xv[2 * ch + 1, row]], axis=1)
             found.append(dot(bk[row], sides.astype(bf16)))
         s1[ch] = pack(found[0], found[1])
+
+    loads[1].wait()
+    wsh[...] = jnp.concatenate([mat[...], jnp.zeros((6, 128), f32)], axis=0).astype(bf16)
+    wz[zme] = wsh[...]
+
+    def analyse_step(ch, carry):
+        analyse(ch)
+
+        @pl.when(ch == 0)
+        def _():
+            pl.semaphore_wait(barrier, LATS - 1 + XS - 1)
+            to_column(wsh, wz.at[zme], 0)
+
+        @pl.when(ch == 2)
+        def _():
+            drain(wz.at[pl.ds(0, 7)], gr.at[0])
+            tiles = wz[...].astype(f32)
+            for z in range(8):
+                wrow[z * 10 : z * 10 + 10, :] = tiles[z, 0:10, :]
+            wb[xme, bme] = wrow[...].astype(bf16)
+            to_plane(lambda other: wb.at[xme, bme], wb.at[xme, bme], 1)
+
+        exchange(0, s1, r1, ch)
         return carry
 
-    lax.fori_loop(0, CH, analyse, 0)
-
-    for number in (1, 2, 3, 7):
+    lax.fori_loop(0, CH, analyse_step, 0)
+
+    for number in (2, 3, 7):
         loads[number].wait()
     sub = lax.broadcasted_iota(jnp.int32, (128, 128), 0)
     lane = lax.broadcasted_iota(jnp.int32, (128, 128), 1)
@@ -355,26 +373,9 @@
     lch[0] = lc_top
     lch[1] = lc_low
 
-    wsh[...] = jnp.concatenate([mat[...], jnp.zeros((6, 128), f32)], axis=0).astype(bf16)
-    wz[zme] = wsh[...]
-    pl.semaphore_wait(barrier, LATS - 1 + XS - 1)
-    to_column(wsh, wz.at[zme], 0)
-    exchange(0, s1, r1, 0)
-    exchange(0, s1, r1, 1)
-
-    drain(wz.at[pl.ds(0, 7)], gr.at[0])
-    tiles = wz[...].astype(f32)
-    for z in range(8):
-        wrow[z * 10 : z * 10 + 10, :] = tiles[z, 0:10, :]
-    wb[xme, bme] = wrow[...].astype(bf16)
-    to_plane(lambda other: wb.at[xme, bme], wb.at[xme, bme], 1)
-    exchange(0, s1, r1, 2)
-
     drain(wb.at[0, pl.ds(0, 7)], gr.at[1])
     own_part = wb.at[xme, pl.ds(4 * odd, 4)]
     to_line(lambda other: own_part, own_part, 2)
-    exchange(0, s1, r1, 3)
-
     drain(wb.at[pl.ds(0, 3), pl.ds(0, 4)], gr.at[2])
     for step in range(1, XS):
         part = wb.at[lax.rem(xme + step, XS), pl.ds(4 * odd, 4)]
@@ -474,14 +475,6 @@
 
     loads[5].wait()
     loads[6].wait()
-    out_copy = [
-        lambda ch: pltpu.make_async_copy(
-            ov.at[pl.ds(2 * ch, 2)], so_hbm.at[pl.ds(2 * ch, 2)], osem.at[0, ch]
-        ),
-        lambda ch: pltpu.make_async_copy(
-            gv.at[pl.ds(2 * ch, 2)], sg_hbm.at[pl.ds(2 * ch, 2)], osem.at[1, ch]
-        ),
-    ]
     c_zero = math.sqrt(2.0 / math.pi)
     c_one = 0.044715
 
@@ -541,7 +534,6 @@
             return carry
 
         lax.fori_loop(0, 2, block, 0)
-        out_copy[0](ch).start()
         s3[ch] = pack(ff[0], ff[1])
         exchange(2, s3, r3, ch)
 
@@ -721,7 +713,6 @@
             grid = dot(bi[row], unpack(r4[ch], row))
             gv[2 * ch, row] = grid[:, 0:128]
             gv[2 * ch + 1, row] = grid[:, 128:256]
-        out_copy[1](ch).start()
 
         @pl.when(ch == 0)
         def _():
@@ -765,12 +756,6 @@
     fin[0:16, :] = bias_total * both_clip
     fin[16:24, :] = norm
     blk[...] = blk[...] * both_clip
-    last = [
-        pltpu.make_async_copy(blk, blk_hbm, isem.at[7]),
-        pltpu.make_async_copy(fin, fin_hbm, isem.at[8]),
-    ]
-    for copy in last:
-        copy.start()
 
     for phase, src in enumerate((s1, s2, s3, s4)):
         for ch in range(CH):
@@ -789,22 +774,78 @@
     drain(pzr.at[pl.ds(0, 7)], gs.at[9])
     drain(pzlr.at[pl.ds(0, 7)], gs.at[13])
     drain(pgr.at[pl.ds(0, 7)], gs.at[10])
-    for ch in range(CH):
-        out_copy[0](ch).wait()
-        out_copy[1](ch).wait()
-    for copy in last:
-        copy.wait()
-
-
-def adam_update(weights, moment, second, grads, steps_done):
+
+
+def adam_update(weights, moment, second, grads, lost_one, lost_two):
     moment_new = beta_one * moment + (1.0 - beta_one) * grads
     second_new = beta_two * second + (1.0 - beta_two) * grads * grads
-    moment_hat = moment_new / (1.0 - beta_one**steps_done)
-    second_hat = second_new / (1.0 - beta_two**steps_done)
+    moment_hat = moment_new / lost_one
+    second_hat = second_new / lost_two
     weights_new = weights - learn_rate * (
         moment_hat / (jnp.sqrt(second_hat) + adam_eps) + decay_rate * weights
     )
     return (weights_new, moment_new, second_new)
+
+
+def update_kernel(
+    so_in,
+    sg_in,
+    blk,
+    fin,
+    mat,
+    mat_m,
+    mat_s,
+    bias,
+    bias_m,
+    bias_s,
+    steps,
+    so_out,
+    sg_out,
+    mat_grad,
+    mat_new,
+    mat_copy,
+    mat_m_new,
+    mat_s_new,
+    bias_grad,
+    bias_new,
+    bias_m_new,
+    bias_s_new,
+    norm,
+    sems,
+):
+    def piece(number):
+        which, part = number % 2, pl.ds(2 * (number // 2), 2)
+        return pltpu.make_async_copy(
+            (so_in, sg_in)[which].at[part], (so_out, sg_out)[which].at[part], sems.at[number]
+        )
+
+    for number in range(2 * CH):
+        piece(number).start()
+    count = jnp.full((1, 128), steps[0], jnp.int32).astype(f32)
+    lost_one = 1.0 - jnp.exp(count * math.log(beta_one))
+    lost_two = 1.0 - jnp.exp(count * math.log(beta_two))
+    block = blk[...]
+    place = 2 * lax.rem(lax.axis_index("lat"), 4)
+    grads = jnp.zeros((10, 128), f32)
+    for begin in (0, 2, 4, 6):
+        grads = jnp.where(place == begin, block[begin : begin + 10], grads)
+    mat_grad[...] = grads
+    new, moment, second = adam_update(mat[...], mat_m[...], mat_s[...], grads, lost_one, lost_two)
+    mat_new[...] = new
+    mat_copy[...] = new.astype(bf16)
+    mat_m_new[...] = moment
+    mat_s_new[...] = second
+    grads = fin[0:BIAS_ROWS, :]
+    bias_grad[...] = grads
+    new, moment, second = adam_update(
+        bias[...], bias_m[...], bias_s[...], grads, lost_one, lost_two
+    )
+    bias_new[...] = new
+    bias_m_new[...] = moment
+    bias_s_new[...] = second
+    norm[0] = jnp.max(fin[16:17, :])
+    for number in range(2 * CH):
+        piece(number).wait()
 
 
 def local(
@@ -829,8 +870,6 @@
     scratch = [
         vm(big, f32),
         vm(big, bf16),
-        vm(big, f32),
-        vm(big, f32),
         vm(big, f32),
         vm((10, 128), f32),
         vm((16, 128), bf16),
@@ -873,7 +912,6 @@
         vm((4, 80, 128), f32),
         vm((8, 16, 128), bf16),
         vm((8, 16, 128), bf16),
-        vm((16, 128), f32),
         vm((160, 128), f32),
         vm((8, 32, 128), f32),
         vm((8, 32, 128), f32),
@@ -885,34 +923,16 @@
         vm((8, 16, 128), bf16),
         vm((24, 128), f32),
         vm((8, 24, 128), f32),
-        vm((24, 128), f32),
         pltpu.SemaphoreType.DMA((CH,)),
         pltpu.SemaphoreType.DMA((10,)),
-        pltpu.SemaphoreType.DMA((2, CH)),
         pltpu.SemaphoreType.DMA((4, CH)),
         pltpu.SemaphoreType.DMA((4, CH)),
         pltpu.SemaphoreType.DMA((14,)),
         pltpu.SemaphoreType.DMA((14,)),
     ]
-    state_out, state_grad, block, final = pl.pallas_call(
-        kernel,
-        out_shape=(
-            jax.ShapeDtypeStruct(big, f32),
-            jax.ShapeDtypeStruct(big, f32),
-            jax.ShapeDtypeStruct((16, 128), f32),
-            jax.ShapeDtypeStruct((24, 128), f32),
-        ),
-        in_specs=[any_spec] * 9,
-        out_specs=(any_spec,) * 4,
-        scratch_shapes=scratch,
-        compiler_params=pltpu.CompilerParams(
-            collective_id=0, has_side_effects=True, vmem_limit_bytes=60 * 1024 * 1024
-        ),
-        cost_estimate=pl.CostEstimate(
-            flops=16 * 10**9, bytes_accessed=10 * 2**20, transcendentals=4 * 10**6
-        ),
-        name="column_step",
-    )(
+    vm_spec = pl.BlockSpec(memory_space=pltpu.VMEM)
+    sm_spec = pl.BlockSpec(memory_space=pltpu.SMEM)
+    operands = (
         state,
         forcing,
         state_cot,
@@ -923,31 +943,56 @@
         jnp.asarray(both),
         jnp.asarray(turned),
     )
-
-    bias_grad = final[0:BIAS_ROWS].reshape(-1)
-    place = 2 * lax.rem(lax.axis_index("lat"), 4)
-    mat_grad = lax.dynamic_slice(block, (place, 0), (10, 128)).reshape(-1)
-    steps_done = step_count[0].astype(f32)
-    mat_new, mat_moment_new, mat_second_new = adam_update(
-        mat_master, mat_moment, mat_second, mat_grad, steps_done
+    held = pl.pallas_call(
+        kernel,
+        out_shape=(vm(big, f32), vm(big, f32), vm((16, 128), f32), vm((24, 128), f32)),
+        in_specs=[any_spec] * 9,
+        out_specs=(vm_spec,) * 4,
+        scratch_shapes=scratch,
+        compiler_params=pltpu.CompilerParams(
+            collective_id=0, has_side_effects=True, vmem_limit_bytes=56 * 1024 * 1024
+        ),
+        cost_estimate=pl.CostEstimate(
+            flops=16 * 10**9, bytes_accessed=10 * 2**20, transcendentals=4 * 10**6
+        ),
+        name="column_step",
+    )(*[pltpu.with_memory_space_constraint(part, pltpu.HBM) for part in operands])
+
+    mat_shape = jax.ShapeDtypeStruct((10, 128), f32)
+    bias_shape = jax.ShapeDtypeStruct((BIAS_ROWS, 128), f32)
+    results = pl.pallas_call(
+        update_kernel,
+        out_shape=(
+            jax.ShapeDtypeStruct(big, f32),
+            jax.ShapeDtypeStruct(big, f32),
+            mat_shape,
+            mat_shape,
+            jax.ShapeDtypeStruct((10, 128), bf16),
+            mat_shape,
+            mat_shape,
+            bias_shape,
+            bias_shape,
+            bias_shape,
+            bias_shape,
+            jax.ShapeDtypeStruct((1,), f32),
+        ),
+        in_specs=[vm_spec] * 10 + [sm_spec],
+        out_specs=(any_spec,) * 2 + (vm_spec,) * 9 + (sm_spec,),
+        scratch_shapes=[pltpu.SemaphoreType.DMA((2 * CH,))],
+        compiler_params=pltpu.CompilerParams(vmem_limit_bytes=16 * 1024 * 1024),
+        cost_estimate=pl.CostEstimate(flops=10**5, bytes_accessed=8 * 2**20, transcendentals=10**4),
+        name="weight_step",
+    )(
+        *[pltpu.with_memory_space_constraint(part, pltpu.VMEM) for part in held],
+        mat_master.reshape(10, 128),
+        mat_moment.reshape(10, 128),
+        mat_second.reshape(10, 128),
+        bias_master.reshape(BIAS_ROWS, 128),
+        bias_moment.reshape(BIAS_ROWS, 128),
+        bias_second.reshape(BIAS_ROWS, 128),
+        step_count,
     )
-    bias_new, bias_moment_new, bias_second_new = adam_update(
-        bias_master, bias_moment, bias_second, bias_grad, steps_done
-    )
-    return (
-        state_out,
-        state_grad,
-        mat_grad,
-        mat_new,
-        mat_new.astype(bf16),
-        mat_moment_new,
-        mat_second_new,
-        bias_grad,
-        bias_new,
-        bias_moment_new,
-        bias_second_new,
-        final[16, 0:1],
-    )
+    return results[0:2] + tuple(part.reshape(-1) for part in results[2:])
 
 
 def solution(mesh):

time: 122 us -> 115 us (0.943)
  local copies, waits for them, and re-layouts: 5.79 us -> 0.03 us
  other arithmetic: 2.67 us -> 0 us
    unnamed x16 -> x12, local copies, waits for them, and re-layouts: 4.61 us -> 0.03 us
    convert_element_type x1 -> x0, other arithmetic: 1.34 us -> none  [local(): mat_new.astype(bf16)]
    sub x1 -> x0, other arithmetic: 1.33 us -> none  [adam_update(): weights - learn_rate * (moment_hat / (jnp.sqrt(second_hat) + adam_eps) +...]
    pallas_call x1 -> x2, Pallas kernels: 112 us -> 113 us  [the longest x1 111 us: local(): pl.pallas_call(kernel, out_shape=(vm(big, f32), vm(big, f32), vm((16, 128...]
where the time goes in v3:
time: 115 us
  Pallas kernels  113 us (98%)
  between operations  1.4 us (1%)
    pallas_call x1, Pallas kernels, local(): pl.pallas_call(kernel, out_shape=(vm(big, f32), vm(big, f32), vm((16, 128...  111 us
    pallas_call x1, Pallas kernels, local(): pl.pallas_call(update_kernel, out_shape=(jax.ShapeDtypeStruct(big, f32),...  2.74 us

profile of v3, /device:TPU:1, one launch (start us, length us, event | category | flops | bytes accessed | tf_op | source)
XLA Modules:
  0.0 114.7 jit_solution(1372234415937930358)
XLA Ops:
  1.3 0.0 copy-start
  1.3 0.0 copy-start.1
  1.3 0.0 copy-start.2
  1.3 0.0 copy-start.3
  1.3 0.0 copy-start.4
  1.3 0.0 copy-start.5
  1.4 110.6 %column_step.1 = (f32[8,2,256,128]{3,2,1,0:T(8,128)S(1)}, f32[8,2,256,128]{3,2,1,0:T(8,128)S(1)}, f32[16,128]{1,0:T(8,128)S(1)}, f32[24,128]{1,0:T(8,128)S(1)}) custom-call(f32[8,2,256,128]{3,2,1,0:T(8,128)} %x_hbm.1, bf16[8,2,256,128]{3,2,1,0:T(8,128)(2,1)} %frc_hbm.1, f32[8,2,256,128]{3,2,1,0:T(8,128)} %cot_hbm.1, f32[10,128]{1,0:T(8,128)} %bitcast.16, ...), custom_call_target="tpu_custom_call" | custom-call | flops 16000000000 | bytes 10485760 | tf_op jit(solution)/shard_map/column_step/pallas_call | solution.py:946
  111.9 0.0 copy-done
  111.9 0.0 copy-done.1
  111.9 0.0 copy-done.2
  112.0 0.0 copy-done.3
  112.0 0.0 copy-done.4
  112.0 0.0 copy-done.5
  112.0 2.7 %weight_step.1 = (f32[8,2,256,128]{3,2,1,0:T(8,128)}, f32[8,2,256,128]{3,2,1,0:T(8,128)}, f32[10,128]{1,0:T(8,128)}, f32[10,128]{1,0:T(8,128)}, bf16[10,128]{1,0...) custom-call(f32[8,2,256,128]{3,2,1,0:T(8,128)S(1)} %get-tuple-elemen, ...), custom_call_target="tpu_custom_call" | custom-call | flops 100000 | bytes 8388608 | tf_op jit(solution)/shard_map/weight_step/pallas_call | solution.py:963
Async XLA Ops:
  1.3 110.6 %copy-start = (f32[1280]{0:T(1024)S(1)}, f32[1280]{0:T(1024)}, u32[]{:S(2)}) copy-start(f32[1280]{0:T(1024)} %param.17) | copy-start | bytes 15364
  1.3 110.6 %copy-start.1 = (f32[1408]{0:T(1024)S(1)}, f32[1408]{0:T(1024)}, u32[]{:S(2)}) copy-start(f32[1408]{0:T(1024)} %param.20) | copy-start | bytes 16900
  1.3 110.6 %copy-start.2 = (f32[1280]{0:T(1024)S(1)}, f32[1280]{0:T(1024)}, u32[]{:S(2)}) copy-start(f32[1280]{0:T(1024)} %param.18) | copy-start | bytes 15364
  1.3 110.6 %copy-start.3 = (f32[1280]{0:T(1024)S(1)}, f32[1280]{0:T(1024)}, u32[]{:S(2)}) copy-start(f32[1280]{0:T(1024)} %param.19) | copy-start | bytes 15364
  1.3 110.6 %copy-start.4 = (f32[1408]{0:T(1024)S(1)}, f32[1408]{0:T(1024)}, u32[]{:S(2)}) copy-start(f32[1408]{0:T(1024)} %param.21) | copy-start | bytes 16900
  1.3 110.6 %copy-start.5 = (f32[1408]{0:T(1024)S(1)}, f32[1408]{0:T(1024)}, u32[]{:S(2)}) copy-start(f32[1408]{0:T(1024)} %param.22) | copy-start | bytes 16900

commit v4 on v3

--- a/solution.py
+++ b/solution.py
@@ -154,6 +154,20 @@
     yme = lax.div(bme, 2)
     odd = lax.rem(me, 2)
 
+    barrier = pltpu.get_barrier_semaphore()
+
+    def greet(step, carry):
+        pl.semaphore_signal(
+            barrier, inc=1, device_id={"lat": lax.rem(me + LATS - step, LATS)}, device_id_type=MESH
+        )
+        return carry
+
+    lax.fori_loop(1, LATS, greet, 0)
+    for step in range(1, XS):
+        pl.semaphore_signal(
+            barrier, inc=1, device_id={"dp": lax.rem(xme + step, XS)}, device_id_type=MESH
+        )
+
     def x_copy(ch):
         part = pl.ds(2 * ch, 2)
         return pltpu.make_async_copy(x_hbm.at[part], xv.at[part], xsem.at[ch])
@@ -174,20 +188,6 @@
     for load in loads[1:]:
         load.start()
 
-    barrier = pltpu.get_barrier_semaphore()
-
-    def greet(step, carry):
-        pl.semaphore_signal(
-            barrier, inc=1, device_id={"lat": lax.rem(me + step, LATS)}, device_id_type=MESH
-        )
-        return carry
-
-    lax.fori_loop(1, LATS, greet, 0)
-    for step in range(1, XS):
-        pl.semaphore_signal(
-            barrier, inc=1, device_id={"dp": lax.rem(xme + step, XS)}, device_id_type=MESH
-        )
-
     sub8 = lax.broadcasted_iota(jnp.int32, (LATS // 2, 8, 128), 1)
     lower = sub8 < 4
 
@@ -216,7 +216,7 @@
 
     def exchange(phase, src, dst, ch):
         def one(step, carry):
-            peer = lax.rem(me + 9 * step, LATS)
+            peer = lax.rem(me + LATS - step, LATS)
             lat_copy(
                 src.at[ch, peer], dst.at[ch, me], ssem.at[phase, ch], rsem.at[phase, ch], peer
             ).start()
@@ -419,7 +419,7 @@
 
     def gather_rows(tiles, slot):
         if slot == 0:
-            rows[...] = tiles.astype(f32).reshape(1024, 128)
+            rows[0:1024, :] = tiles.astype(f32).reshape(1024, 128)
         sides = []
         for globe in range(2):
             for part in range(2):
@@ -450,7 +450,7 @@
                         rows[pl.ds(begin + 4 * k, LATS, stride=16), :] = found[
                             k * LATS : k * LATS + LATS, lanes
                         ]
-        return rows[...].astype(bf16).reshape(LATS, 16, 128)
+        return rows[0:1024, :].astype(bf16).reshape(LATS, 16, 128)
 
     def cut(value):
         return [value[c * 128 : c * 128 + 128] for c in range(8)]
@@ -500,10 +500,11 @@
                 square = pre * pre
                 inner = pre * (c_zero + (c_zero * c_one) * square)
                 bent = jnp.tanh(inner)
-                half = 0.5 * pre
-                hidden = (half + half * bent).astype(bf16)
-                slope = half * (c_zero + (3.0 * c_zero * c_one) * square)
-                gel[layer] = (0.5 + 0.5 * bent) + slope * (1.0 - bent * bent)
+                share = 0.5 + 0.5 * bent
+                active = pre * share
+                hidden = active.astype(bf16)
+                slope = (2.0 * c_zero) + (6.0 * c_zero * c_one) * square
+                gel[layer] = share + active * (slope * (1.0 - share))
                 hid[layer + 1] = hidden
             middle = dynamic + dot(hidden, w5[...]) + bias_row(9, 1)
             middle_low = middle.astype(bf16)
@@ -811,6 +812,16 @@
     bias_m_new,
     bias_s_new,
     norm,
+    mat_grad_v,
+    mat_new_v,
+    mat_copy_v,
+    mat_m_new_v,
+    mat_s_new_v,
+    bias_grad_v,
+    bias_new_v,
+    bias_m_new_v,
+    bias_s_new_v,
+    norm_v,
     sems,
 ):
     def piece(number):
@@ -821,7 +832,7 @@
 
     for number in range(2 * CH):
         piece(number).start()
-    count = jnp.full((1, 128), steps[0], jnp.int32).astype(f32)
+    count = jnp.broadcast_to(steps[...].astype(f32), (1, 128))
     lost_one = 1.0 - jnp.exp(count * math.log(beta_one))
     lost_two = 1.0 - jnp.exp(count * math.log(beta_two))
     block = blk[...]
@@ -829,23 +840,39 @@
     grads = jnp.zeros((10, 128), f32)
     for begin in (0, 2, 4, 6):
         grads = jnp.where(place == begin, block[begin : begin + 10], grads)
-    mat_grad[...] = grads
+    mat_grad_v[...] = grads
     new, moment, second = adam_update(mat[...], mat_m[...], mat_s[...], grads, lost_one, lost_two)
-    mat_new[...] = new
-    mat_copy[...] = new.astype(bf16)
-    mat_m_new[...] = moment
-    mat_s_new[...] = second
+    mat_new_v[...] = new
+    mat_copy_v[...] = new.astype(bf16)
+    mat_m_new_v[...] = moment
+    mat_s_new_v[...] = second
     grads = fin[0:BIAS_ROWS, :]
-    bias_grad[...] = grads
+    bias_grad_v[...] = grads
     new, moment, second = adam_update(
         bias[...], bias_m[...], bias_s[...], grads, lost_one, lost_two
     )
-    bias_new[...] = new
-    bias_m_new[...] = moment
-    bias_s_new[...] = second
-    norm[0] = jnp.max(fin[16:17, :])
+    bias_new_v[...] = new
+    bias_m_new_v[...] = moment
+    bias_s_new_v[...] = second
+    norm_v[...] = fin[16:17, 0:1]
+    small = [
+        pltpu.make_async_copy(mat_grad_v, mat_grad, sems.at[8]),
+        pltpu.make_async_copy(mat_new_v, mat_new, sems.at[9]),
+        pltpu.make_async_copy(mat_copy_v, mat_copy, sems.at[10]),
+        pltpu.make_async_copy(mat_m_new_v, mat_m_new, sems.at[11]),
+        pltpu.make_async_copy(mat_s_new_v, mat_s_new, sems.at[12]),
+        pltpu.make_async_copy(bias_grad_v, bias_grad, sems.at[13]),
+        pltpu.make_async_copy(bias_new_v, bias_new, sems.at[14]),
+        pltpu.make_async_copy(bias_m_new_v, bias_m_new, sems.at[15]),
+        pltpu.make_async_copy(bias_s_new_v, bias_s_new, sems.at[16]),
+        pltpu.make_async_copy(norm_v, norm, sems.at[17]),
+    ]
+    for copy in small:
+        copy.start()
     for number in range(2 * CH):
         piece(number).wait()
+    for copy in small:
+        copy.wait()
 
 
 def local(
@@ -880,7 +907,7 @@
         vm((2, 256, 256), bf16),
         *[vm(tiles, bf16) for _ in range(8)],
         *[vm((2, 128, 128), bf16) for _ in range(4)],
-        vm((1024, 128), f32),
+        vm((1040, 128), f32),
         vm((CH, 1024, 128), bf16),
         vm((2, 128, 128), f32),
         vm((2, 2, 128, 128), f32),
@@ -931,7 +958,6 @@
         pltpu.SemaphoreType.DMA((14,)),
     ]
     vm_spec = pl.BlockSpec(memory_space=pltpu.VMEM)
-    sm_spec = pl.BlockSpec(memory_space=pltpu.SMEM)
     operands = (
         state,
         forcing,
@@ -974,11 +1000,17 @@
             bias_shape,
             bias_shape,
             bias_shape,
-            jax.ShapeDtypeStruct((1,), f32),
+            jax.ShapeDtypeStruct((1, 1), f32),
         ),
-        in_specs=[vm_spec] * 10 + [sm_spec],
-        out_specs=(any_spec,) * 2 + (vm_spec,) * 9 + (sm_spec,),
-        scratch_shapes=[pltpu.SemaphoreType.DMA((2 * CH,))],
+        in_specs=[vm_spec] * 11,
+        out_specs=(any_spec,) * 12,
+        scratch_shapes=[
+            *[vm((10, 128), f32), vm((10, 128), f32), vm((10, 128), bf16)],
+            *[vm((10, 128), f32) for _ in range(2)],
+            *[vm((BIAS_ROWS, 128), f32) for _ in range(4)],
+            vm((1, 1), f32),
+            pltpu.SemaphoreType.DMA((2 * CH + 10,)),
+        ],
         compiler_params=pltpu.CompilerParams(vmem_limit_bytes=16 * 1024 * 1024),
         cost_estimate=pl.CostEstimate(flops=10**5, bytes_accessed=8 * 2**20, transcendentals=10**4),
         name="weight_step",
@@ -990,7 +1022,7 @@
         bias_master.reshape(BIAS_ROWS, 128),
         bias_moment.reshape(BIAS_ROWS, 128),
         bias_second.reshape(BIAS_ROWS, 128),
-        step_count,
+        step_count.reshape(1, 1),
     )
     return results[0:2] + tuple(part.reshape(-1) for part in results[2:])
 

time: 115 us -> 113 us (0.983)
  no operation moved by 1% of the time
where the time goes in v4:
time: 113 us
  Pallas kernels  112 us (99%)
  between operations  1.4 us (1%)
    pallas_call x1, Pallas kernels, local(): pl.pallas_call(kernel, out_shape=(vm(big, f32), vm(big, f32), vm((16, 128...  109 us

profile of v4, /device:TPU:1, one launch (start us, length us, event | category | flops | bytes accessed | tf_op | source)
XLA Modules:
  0.0 113.1 jit_solution(1486155994468363813)
XLA Ops:
  1.3 0.0 copy-start
  1.3 0.0 copy-start.1
  1.3 0.0 copy-start.2
  1.3 0.0 copy-start.3
  1.3 0.0 copy-start.4
  1.3 0.0 copy-start.5
  1.4 109.4 %column_step.1 = (f32[8,2,256,128]{3,2,1,0:T(8,128)S(1)}, f32[8,2,256,128]{3,2,1,0:T(8,128)S(1)}, f32[16,128]{1,0:T(8,128)S(1)}, f32[24,128]{1,0:T(8,128)S(1)}) custom-call(f32[8,2,256,128]{3,2,1,0:T(8,128)} %x_hbm.1, bf16[8,2,256,128]{3,2,1,0:T(8,128)(2,1)} %frc_hbm.1, f32[8,2,256,128]{3,2,1,0:T(8,128)} %cot_hbm.1, f32[10,128]{1,0:T(8,128)} %bitcast.19, ...), custom_call_target="tpu_custom_call" | custom-call | flops 16000000000 | bytes 10485760 | tf_op jit(solution)/shard_map/column_step/pallas_call | solution.py:972
  110.8 0.0 copy-done
  110.8 0.0 copy-done.1
  110.8 0.0 copy-done.2
  110.8 0.0 copy-done.3
  110.8 0.0 copy-done.4
  110.9 0.0 copy-done.5
  110.9 2.2 %weight_step.1 = (f32[8,2,256,128]{3,2,1,0:T(8,128)}, f32[8,2,256,128]{3,2,1,0:T(8,128)}, f32[10,128]{1,0:T(8,128)}, f32[10,128]{1,0:T(8,128)}, bf16[10,128]{1,0...) custom-call(f32[8,2,256,128]{3,2,1,0:T(8,128)S(1)} %get-tuple-elemen, ...), custom_call_target="tpu_custom_call" | custom-call | flops 100000 | bytes 8388608 | tf_op jit(solution)/shard_map/weight_step/pallas_call | solution.py:989
Async XLA Ops:
  1.3 109.5 %copy-start = (f32[1280]{0:T(1024)S(1)}, f32[1280]{0:T(1024)}, u32[]{:S(2)}) copy-start(f32[1280]{0:T(1024)} %param.17) | copy-start | bytes 15364
  1.3 109.5 %copy-start.1 = (f32[1408]{0:T(1024)S(1)}, f32[1408]{0:T(1024)}, u32[]{:S(2)}) copy-start(f32[1408]{0:T(1024)} %param.20) | copy-start | bytes 16900
  1.3 109.5 %copy-start.2 = (f32[1280]{0:T(1024)S(1)}, f32[1280]{0:T(1024)}, u32[]{:S(2)}) copy-start(f32[1280]{0:T(1024)} %param.18) | copy-start | bytes 15364
  1.3 109.5 %copy-start.3 = (f32[1280]{0:T(1024)S(1)}, f32[1280]{0:T(1024)}, u32[]{:S(2)}) copy-start(f32[1280]{0:T(1024)} %param.19) | copy-start | bytes 15364
  1.3 109.5 %copy-start.4 = (f32[1408]{0:T(1024)S(1)}, f32[1408]{0:T(1024)}, u32[]{:S(2)}) copy-start(f32[1408]{0:T(1024)} %param.21) | copy-start | bytes 16900
  1.3 109.5 %copy-start.5 = (f32[1408]{0:T(1024)S(1)}, f32[1408]{0:T(1024)}, u32[]{:S(2)}) copy-start(f32[1408]{0:T(1024)} %param.22) | copy-start | bytes 16900

commit v5 on v4

--- a/solution.py
+++ b/solution.py
@@ -153,6 +153,8 @@
     bme = lax.rem(me, 8)
     yme = lax.div(bme, 2)
     odd = lax.rem(me, 2)
+    parity = lax.rem(odd + zme, 2)
+    turn = lax.div(odd + zme, 2)
 
     barrier = pltpu.get_barrier_semaphore()
 
@@ -560,7 +562,7 @@
         gf[2432:2560, :] = dwd[...]
 
         def one(part, carry):
-            begin = pl.multiple_of(part * 160 + 80 * (1 - odd), 8)
+            begin = pl.multiple_of(part * 160 + 80 * (1 - parity), 8)
             lat_copy(
                 gf.at[pl.ds(begin, 80)], rk.at[part], gs.at[12], gr.at[12], me + 1 - 2 * odd
             ).start()
@@ -572,7 +574,7 @@
         drain(rk, gr.at[12])
 
         def one(part, carry):
-            begin = pl.multiple_of(part * 160 + 80 * odd, 8)
+            begin = pl.multiple_of(part * 160 + 80 * parity, 8)
             total = rk[part] + gf[pl.ds(begin, 80), :]
             rk[part] = total
             rh[part] = total.astype(bf16)
@@ -590,11 +592,13 @@
         for step in range(1, 4):
             other = lax.rem(yme + step, 4)
             peer = zme * 8 + other * 2 + odd
-            lat_copy(s1r.at[other], ry.at[yme], gs.at[4], gr.at[4], peer).start()
+            lat_copy(
+                s1r.at[lax.rem(other + turn, 4)], ry.at[yme], gs.at[4], gr.at[4], peer
+            ).start()
 
     def grad_column():
         drain(ry.at[pl.ds(0, 3)], gr.at[4])
-        total = s1r[yme]
+        total = s1r[lax.rem(yme + turn, 4)]
         for step in range(1, 4):
             total = total + ry[lax.rem(yme + step, 4)]
         for b in range(8):
@@ -602,7 +606,7 @@
             s2r[b] = total[begin : begin + 16].astype(bf16)
         for step in range(8):
             other = lax.rem(bme + step, 8)
-            peer = bme * 8 + other
+            peer = lax.rem(bme + zme, 8) * 8 + other
 
             @pl.when(peer != me)
             def _():
@@ -615,11 +619,11 @@
                 rw[zme] = s2r[other]
 
     def turn_bytes(sem):
-        @pl.when(bme == zme)
+        @pl.when(bme == 0)
         def _():
             drain(rw.at[pl.ds(0, 7)], sem)
 
-        @pl.when(bme != zme)
+        @pl.when(bme != 0)
         def _():
             drain(rw, sem)
 

time: 113 us -> 112 us (level)
  no operation moved by 1% of the time
where the time goes in v5:
time: 112 us
  Pallas kernels  111 us (99%)
  between operations  1.4 us (1%)
    pallas_call x1, Pallas kernels, local(): pl.pallas_call(kernel, out_shape=(vm(big, f32), vm(big, f32), vm((16, 128...  109 us

profile of v5, /device:TPU:1, one launch (start us, length us, event | category | flops | bytes accessed | tf_op | source)
XLA Modules:
  0.0 112.3 jit_solution(15564781687046244390)
XLA Ops:
  1.3 0.0 copy-start
  1.3 0.0 copy-start.1
  1.3 0.0 copy-start.2
  1.3 0.0 copy-start.3
  1.3 0.0 copy-start.4
  1.3 0.0 copy-start.5
  1.4 108.6 %column_step.1 = (f32[8,2,256,128]{3,2,1,0:T(8,128)S(1)}, f32[8,2,256,128]{3,2,1,0:T(8,128)S(1)}, f32[16,128]{1,0:T(8,128)S(1)}, f32[24,128]{1,0:T(8,128)S(1)}) custom-call(f32[8,2,256,128]{3,2,1,0:T(8,128)} %x_hbm.1, bf16[8,2,256,128]{3,2,1,0:T(8,128)(2,1)} %frc_hbm.1, f32[8,2,256,128]{3,2,1,0:T(8,128)} %cot_hbm.1, f32[10,128]{1,0:T(8,128)} %bitcast.19, ...), custom_call_target="tpu_custom_call" | custom-call | flops 16000000000 | bytes 10485760 | tf_op jit(solution)/shard_map/column_step/pallas_call | solution.py:976
  110.0 0.0 copy-done
  110.0 0.0 copy-done.1
  110.0 0.0 copy-done.2
  110.0 0.0 copy-done.3
  110.0 0.0 copy-done.4
  110.0 0.0 copy-done.5
  110.1 2.2 %weight_step.1 = (f32[8,2,256,128]{3,2,1,0:T(8,128)}, f32[8,2,256,128]{3,2,1,0:T(8,128)}, f32[10,128]{1,0:T(8,128)}, f32[10,128]{1,0:T(8,128)}, bf16[10,128]{1,0...) custom-call(f32[8,2,256,128]{3,2,1,0:T(8,128)S(1)} %get-tuple-elemen, ...), custom_call_target="tpu_custom_call" | custom-call | flops 100000 | bytes 8388608 | tf_op jit(solution)/shard_map/weight_step/pallas_call | solution.py:993
Async XLA Ops:
  1.3 108.7 %copy-start = (f32[1280]{0:T(1024)S(1)}, f32[1280]{0:T(1024)}, u32[]{:S(2)}) copy-start(f32[1280]{0:T(1024)} %param.17) | copy-start | bytes 15364
  1.3 108.7 %copy-start.1 = (f32[1408]{0:T(1024)S(1)}, f32[1408]{0:T(1024)}, u32[]{:S(2)}) copy-start(f32[1408]{0:T(1024)} %param.20) | copy-start | bytes 16900
  1.3 108.7 %copy-start.2 = (f32[1280]{0:T(1024)S(1)}, f32[1280]{0:T(1024)}, u32[]{:S(2)}) copy-start(f32[1280]{0:T(1024)} %param.18) | copy-start | bytes 15364
  1.3 108.7 %copy-start.3 = (f32[1280]{0:T(1024)S(1)}, f32[1280]{0:T(1024)}, u32[]{:S(2)}) copy-start(f32[1280]{0:T(1024)} %param.19) | copy-start | bytes 15364
  1.3 108.7 %copy-start.4 = (f32[1408]{0:T(1024)S(1)}, f32[1408]{0:T(1024)}, u32[]{:S(2)}) copy-start(f32[1408]{0:T(1024)} %param.21) | copy-start | bytes 16900
  1.3 108.7 %copy-start.5 = (f32[1408]{0:T(1024)S(1)}, f32[1408]{0:T(1024)}, u32[]{:S(2)}) copy-start(f32[1408]{0:T(1024)} %param.22) | copy-start | bytes 16900
